TPU v7x, 256 devices: a whole 4x4x8 slice. The times are simulated.
256 devices in a mesh: gx: 32 (over x, z), gy: 4 (over y), gz: 2 (over core).
Axes of the slice: x: 4, y: 4, z: 8, core: 2. Of those that a mesh axis runs over, the one named last changes fastest.
Arguments:
- features: float32 [32, 4, 2, 64, 6144], P('gx', 'gy', 'gz'), may hold values from -6 to 6
- boundary_rows: int32 [32, 4, 2, 512], P('gx', 'gy', 'gz'), may hold values from 0 to 6143
- in_maps: int32 [32, 4, 2, 26, 3072], P('gx', 'gy', 'gz'), may hold values from 0 to 19968, as said below
- out_maps: int32 [32, 4, 2, 26, 3072], P('gx', 'gy', 'gz'), may hold values from 0 to 6144, as said below
- send_rows: int32 [32, 4, 2, 32, 384], P('gx', 'gy', 'gz'), may hold values from 0 to 6144, as said below
- recv_coarse: int32 [32, 4, 2, 32, 384], P('gx', 'gy', 'gz'), may hold values from 0 to 3072, as said below
- conv_weight: float32 [27, 64, 64], replicated, may hold values from -0.25 to 0.25
- scale_one: float32 [64], replicated, may hold values from 0.1 to 1.9
- shift_one: float32 [64], replicated, may hold values from -3 to 3
- down_weight: float32 [8, 128, 64], replicated, may hold values from -0.5 to 0.5
- scale_two: float32 [128], replicated, may hold values from 0.1 to 1.9
- shift_two: float32 [128], replicated, may hold values from -3 to 3
Outputs:
- fine_out: float32 [32, 4, 2, 64, 6144], P('gx', 'gy', 'gz')
- coarse_out: float32 [32, 4, 2, 128, 3072], P('gx', 'gy', 'gz')
Inputs may be any that keep to these rules, and one draw needn't show every extreme that they name: `in_maps`: live entries of a list come first; each names a column of that block's source table: an own row below 6144, or row r of the buffer of a neighbour in position q at 6144 + q * 512 + r, where q's displacement in each dimension is 0 or that of the list's offset and not all 0. Padding entries name the zero column 19968. Every list has 768 or more live entries, and in every draw some lists are full. `out_maps`: live entries of one list name distinct rows of the block and come first, in the same slots as the live entries of in_maps; padding entries are 6144. `send_rows`: each fine row of a block stands in exactly one slot of that block's table; empty slots hold 6144. In every draw each block fills all 384 slots of some owner. `recv_coarse`: entry [s, t] of owner (a, b, c) is 3072 exactly where send_rows of block (s, b, c) holds 6144 for owner a in slot t, else a coarse row below 3072.
All inputs are finite; a program needn't handle non-finite values.
Results may differ from a plain program's by a relative error of at most 0.0003.
Values sent between devices are 32-bit elements; how exact they have to be, the bound alone decides.
No kernel may reach another device: no remote copies, remote signals or barrier semaphores. Data moves between devices by JAX's collectives and lax.ppermute only.
A program may use at most 64 MiB of HBM per device.

v0:
```python
import jax
import jax.numpy as jnp
from jax import lax
from jax.sharding import PartitionSpec as P

COARSE = 3072


HIGH = lax.Precision.HIGHEST


def with_halo(block, sides, width):
    for axis, dim in sides:
        count = lax.axis_size(axis)
        forward = [(i, i + 1) for i in range(count - 1)]
        backward = [(target, source) for source, target in forward]
        low = lax.ppermute(
            lax.slice_in_dim(block, block.shape[dim] - width, None, axis=dim), axis, forward
        )
        high = lax.ppermute(lax.slice_in_dim(block, 0, width, axis=dim), axis, backward)
        block = jnp.concatenate([low, block, high], axis=dim)
    return block


def layer_one(own, near, ins, outs, conv_weight, scale_one, shift_one):
    chans, voxels = own.shape
    source = jnp.concatenate([own, near, jnp.zeros((chans, 1), jnp.float32)], axis=1)
    centre = jnp.dot(conv_weight[13], own, precision=HIGH)
    total = jnp.concatenate([centre, jnp.zeros((chans, 1), jnp.float32)], axis=1)
    others = jnp.concatenate([conv_weight[:13], conv_weight[14:]], axis=0)

    def step(acc, item):
        weight, src_cols, dst_cols = item
        picked = jnp.take(source, src_cols, axis=1)
        return (acc.at[:, dst_cols].add(jnp.dot(weight, picked, precision=HIGH)), None)

    total, unused = lax.scan(step, total, (others, ins, outs))
    return jnp.maximum(scale_one[:, None] * total[:, :voxels] + shift_one[:, None], 0.0)


def body(
    features,
    boundary_rows,
    in_maps,
    out_maps,
    send_rows,
    recv_coarse,
    conv_weight,
    scale_one,
    shift_one,
    down_weight,
    scale_two,
    shift_two,
):
    own = features[0, 0, 0]
    chans, voxels = own.shape
    buffer = jnp.take(own, boundary_rows[0, 0, 0], axis=1)[:, None, None, None, :]
    near = with_halo(buffer, (("gx", 1), ("gy", 2), ("gz", 3)), 1)
    near = near.reshape(chans, -1)
    fine = layer_one(
        own, near, in_maps[0, 0, 0], out_maps[0, 0, 0], conv_weight, scale_one, shift_one
    )
    fine_pad = jnp.concatenate([fine, jnp.zeros((chans, 1), jnp.float32)], axis=1)
    table = send_rows[0, 0, 0]
    owners, slots = table.shape
    packed = jnp.take(fine_pad, table, axis=1).reshape(chans, owners, 8, slots // 8)
    arrived = lax.all_to_all(packed, "gx", split_axis=1, concat_axis=1, tiled=True)
    part = jnp.einsum("omc,cson->mson", down_weight, arrived, precision=HIGH)
    outputs = part.shape[0]
    flat = part.reshape(outputs, -1)
    cols = recv_coarse[0, 0, 0].reshape(-1)
    total = jnp.zeros((outputs, COARSE + 1), jnp.float32).at[:, cols].add(flat)
    coarse = jnp.maximum(scale_two[:, None] * total[:, :COARSE] + shift_two[:, None], 0.0)
    return (fine[None, None, None], coarse[None, None, None])


def solution(mesh):
    return jax.shard_map(
        body,
        mesh=mesh,
        in_specs=(
            P("gx", "gy", "gz", None, None),
            P("gx", "gy", "gz", None),
            P("gx", "gy", "gz", None, None),
            P("gx", "gy", "gz", None, None),
            P("gx", "gy", "gz", None, None),
            P("gx", "gy", "gz", None, None),
            P(),
            P(),
            P(),
            P(),
            P(),
            P(),
        ),
        out_specs=(P("gx", "gy", "gz", None, None), P("gx", "gy", "gz", None, None)),
        check_vma=False,
    )
```

profile of v0, /device:TPU:8, one launch (start us, length us, event | category | flops | bytes accessed | tf_op | source)
XLA Modules:
  0.0 1414.5 jit_solution(10491353694560051010)
XLA Ops:
  65.2 16.4 %maximum_maximum_fusion = f32[64,19969]{0,1:T(8,128)} fusion(f32[64,13824]{0,1:T(8,128)S(1)} %bitcast.73, f32[64,6144]{0,1:T(8,128)S(1)} %bitcast.76, f32[19969]{0:T(1024)S(1)} %pad.4.clone), kind=kLoop, calls=%fused_computation.19 | loop fusion | flops 2556032 | bytes 10303748 | tf_op jit(solution)/shard_map/concatenate | solution.py:27
  81.6 992.8 %while.10 = (s32[]{:T(128)}, f32[64,6145]{0,1:T(8,128)S(1)}, s32[26,3072]{1,0:T(8,128)}, f32[26,64,64]{2,1,0:T(8,128)}, s32[26,3072]{1,0:T(8,128)}, /*index=5*/f32[64,19969]{0,1:T(8,128)}, s32[]{:T(128)}) while((s32[]{:T(128)}, f32[64,6145]{0,1:T(8,128)S(1)}, s32[26,3072]{1,0:T(8,128)}, f32[26,64,64]{2,1,0:T(8,128)}, s32[26,3072]{1,0:T(8,128)}, ...), condition=%wide.region_2.3_spmd, body=%wide.region_0.0_spmd.sunk | while | flops 151428096 | bytes 6453841 | solution.py:37
  101.5 18.3 %scatter_fusion = f32[64,6145]{0,1:T(8,128)S(1)} fusion(f32[64,6145]{0,1:T(8,128)S(1)} %get-tuple-element.129, s32[3072]{0:T(1024)S(1)} %bitcast.82, f32[3072,64]{1,0:T(8,128)} %fusion.31), kind=kCustom, calls=%fused_computation.3.clone.1 | custom fusion | flops 196608 | bytes 2371584 | tf_op jit(solution)/shard_map/while/body/eval_jaxpr/scatter-add | solution.py:35
  139.7 18.3 %scatter_fusion = f32[64,6145]{0,1:T(8,128)S(1)} fusion(f32[64,6145]{0,1:T(8,128)S(1)} %get-tuple-element.129, s32[3072]{0:T(1024)S(1)} %bitcast.82, f32[3072,64]{1,0:T(8,128)} %fusion.31), kind=kCustom, calls=%fused_computation.3.clone.1 | custom fusion | flops 196608 | bytes 2371584 | tf_op jit(solution)/shard_map/while/body/eval_jaxpr/scatter-add | solution.py:35
  177.8 18.3 %scatter_fusion = f32[64,6145]{0,1:T(8,128)S(1)} fusion(f32[64,6145]{0,1:T(8,128)S(1)} %get-tuple-element.129, s32[3072]{0:T(1024)S(1)} %bitcast.82, f32[3072,64]{1,0:T(8,128)} %fusion.31), kind=kCustom, calls=%fused_computation.3.clone.1 | custom fusion | flops 196608 | bytes 2371584 | tf_op jit(solution)/shard_map/while/body/eval_jaxpr/scatter-add | solution.py:35
  216.0 18.3 %scatter_fusion = f32[64,6145]{0,1:T(8,128)S(1)} fusion(f32[64,6145]{0,1:T(8,128)S(1)} %get-tuple-element.129, s32[3072]{0:T(1024)S(1)} %bitcast.82, f32[3072,64]{1,0:T(8,128)} %fusion.31), kind=kCustom, calls=%fused_computation.3.clone.1 | custom fusion | flops 196608 | bytes 2371584 | tf_op jit(solution)/shard_map/while/body/eval_jaxpr/scatter-add | solution.py:35
  254.2 18.3 %scatter_fusion = f32[64,6145]{0,1:T(8,128)S(1)} fusion(f32[64,6145]{0,1:T(8,128)S(1)} %get-tuple-element.129, s32[3072]{0:T(1024)S(1)} %bitcast.82, f32[3072,64]{1,0:T(8,128)} %fusion.31), kind=kCustom, calls=%fused_computation.3.clone.1 | custom fusion | flops 196608 | bytes 2371584 | tf_op jit(solution)/shard_map/while/body/eval_jaxpr/scatter-add | solution.py:35
  292.4 18.3 %scatter_fusion = f32[64,6145]{0,1:T(8,128)S(1)} fusion(f32[64,6145]{0,1:T(8,128)S(1)} %get-tuple-element.129, s32[3072]{0:T(1024)S(1)} %bitcast.82, f32[3072,64]{1,0:T(8,128)} %fusion.31), kind=kCustom, calls=%fused_computation.3.clone.1 | custom fusion | flops 196608 | bytes 2371584 | tf_op jit(solution)/shard_map/while/body/eval_jaxpr/scatter-add | solution.py:35
  330.6 18.3 %scatter_fusion = f32[64,6145]{0,1:T(8,128)S(1)} fusion(f32[64,6145]{0,1:T(8,128)S(1)} %get-tuple-element.129, s32[3072]{0:T(1024)S(1)} %bitcast.82, f32[3072,64]{1,0:T(8,128)} %fusion.31), kind=kCustom, calls=%fused_computation.3.clone.1 | custom fusion | flops 196608 | bytes 2371584 | tf_op jit(solution)/shard_map/while/body/eval_jaxpr/scatter-add | solution.py:35
  368.8 18.3 %scatter_fusion = f32[64,6145]{0,1:T(8,128)S(1)} fusion(f32[64,6145]{0,1:T(8,128)S(1)} %get-tuple-element.129, s32[3072]{0:T(1024)S(1)} %bitcast.82, f32[3072,64]{1,0:T(8,128)} %fusion.31), kind=kCustom, calls=%fused_computation.3.clone.1 | custom fusion | flops 196608 | bytes 2371584 | tf_op jit(solution)/shard_map/while/body/eval_jaxpr/scatter-add | solution.py:35
  406.9 18.3 %scatter_fusion = f32[64,6145]{0,1:T(8,128)S(1)} fusion(f32[64,6145]{0,1:T(8,128)S(1)} %get-tuple-element.129, s32[3072]{0:T(1024)S(1)} %bitcast.82, f32[3072,64]{1,0:T(8,128)} %fusion.31), kind=kCustom, calls=%fused_computation.3.clone.1 | custom fusion | flops 196608 | bytes 2371584 | tf_op jit(solution)/shard_map/while/body/eval_jaxpr/scatter-add | solution.py:35
  445.1 18.3 %scatter_fusion = f32[64,6145]{0,1:T(8,128)S(1)} fusion(f32[64,6145]{0,1:T(8,128)S(1)} %get-tuple-element.129, s32[3072]{0:T(1024)S(1)} %bitcast.82, f32[3072,64]{1,0:T(8,128)} %fusion.31), kind=kCustom, calls=%fused_computation.3.clone.1 | custom fusion | flops 196608 | bytes 2371584 | tf_op jit(solution)/shard_map/while/body/eval_jaxpr/scatter-add | solution.py:35
  483.3 18.3 %scatter_fusion = f32[64,6145]{0,1:T(8,128)S(1)} fusion(f32[64,6145]{0,1:T(8,128)S(1)} %get-tuple-element.129, s32[3072]{0:T(1024)S(1)} %bitcast.82, f32[3072,64]{1,0:T(8,128)} %fusion.31), kind=kCustom, calls=%fused_computation.3.clone.1 | custom fusion | flops 196608 | bytes 2371584 | tf_op jit(solution)/shard_map/while/body/eval_jaxpr/scatter-add | solution.py:35
  521.5 18.3 %scatter_fusion = f32[64,6145]{0,1:T(8,128)S(1)} fusion(f32[64,6145]{0,1:T(8,128)S(1)} %get-tuple-element.129, s32[3072]{0:T(1024)S(1)} %bitcast.82, f32[3072,64]{1,0:T(8,128)} %fusion.31), kind=kCustom, calls=%fused_computation.3.clone.1 | custom fusion | flops 196608 | bytes 2371584 | tf_op jit(solution)/shard_map/while/body/eval_jaxpr/scatter-add | solution.py:35
  559.7 18.3 %scatter_fusion = f32[64,6145]{0,1:T(8,128)S(1)} fusion(f32[64,6145]{0,1:T(8,128)S(1)} %get-tuple-element.129, s32[3072]{0:T(1024)S(1)} %bitcast.82, f32[3072,64]{1,0:T(8,128)} %fusion.31), kind=kCustom, calls=%fused_computation.3.clone.1 | custom fusion | flops 196608 | bytes 2371584 | tf_op jit(solution)/shard_map/while/body/eval_jaxpr/scatter-add | solution.py:35
  597.9 18.3 %scatter_fusion = f32[64,6145]{0,1:T(8,128)S(1)} fusion(f32[64,6145]{0,1:T(8,128)S(1)} %get-tuple-element.129, s32[3072]{0:T(1024)S(1)} %bitcast.82, f32[3072,64]{1,0:T(8,128)} %fusion.31), kind=kCustom, calls=%fused_computation.3.clone.1 | custom fusion | flops 196608 | bytes 2371584 | tf_op jit(solution)/shard_map/while/body/eval_jaxpr/scatter-add | solution.py:35
  636.0 18.3 %scatter_fusion = f32[64,6145]{0,1:T(8,128)S(1)} fusion(f32[64,6145]{0,1:T(8,128)S(1)} %get-tuple-element.129, s32[3072]{0:T(1024)S(1)} %bitcast.82, f32[3072,64]{1,0:T(8,128)} %fusion.31), kind=kCustom, calls=%fused_computation.3.clone.1 | custom fusion | flops 196608 | bytes 2371584 | tf_op jit(solution)/shard_map/while/body/eval_jaxpr/scatter-add | solution.py:35
  674.2 18.3 %scatter_fusion = f32[64,6145]{0,1:T(8,128)S(1)} fusion(f32[64,6145]{0,1:T(8,128)S(1)} %get-tuple-element.129, s32[3072]{0:T(1024)S(1)} %bitcast.82, f32[3072,64]{1,0:T(8,128)} %fusion.31), kind=kCustom, calls=%fused_computation.3.clone.1 | custom fusion | flops 196608 | bytes 2371584 | tf_op jit(solution)/shard_map/while/body/eval_jaxpr/scatter-add | solution.py:35
  712.4 18.3 %scatter_fusion = f32[64,6145]{0,1:T(8,128)S(1)} fusion(f32[64,6145]{0,1:T(8,128)S(1)} %get-tuple-element.129, s32[3072]{0:T(1024)S(1)} %bitcast.82, f32[3072,64]{1,0:T(8,128)} %fusion.31), kind=kCustom, calls=%fused_computation.3.clone.1 | custom fusion | flops 196608 | bytes 2371584 | tf_op jit(solution)/shard_map/while/body/eval_jaxpr/scatter-add | solution.py:35
  750.6 18.3 %scatter_fusion = f32[64,6145]{0,1:T(8,128)S(1)} fusion(f32[64,6145]{0,1:T(8,128)S(1)} %get-tuple-element.129, s32[3072]{0:T(1024)S(1)} %bitcast.82, f32[3072,64]{1,0:T(8,128)} %fusion.31), kind=kCustom, calls=%fused_computation.3.clone.1 | custom fusion | flops 196608 | bytes 2371584 | tf_op jit(solution)/shard_map/while/body/eval_jaxpr/scatter-add | solution.py:35
  788.8 18.3 %scatter_fusion = f32[64,6145]{0,1:T(8,128)S(1)} fusion(f32[64,6145]{0,1:T(8,128)S(1)} %get-tuple-element.129, s32[3072]{0:T(1024)S(1)} %bitcast.82, f32[3072,64]{1,0:T(8,128)} %fusion.31), kind=kCustom, calls=%fused_computation.3.clone.1 | custom fusion | flops 196608 | bytes 2371584 | tf_op jit(solution)/shard_map/while/body/eval_jaxpr/scatter-add | solution.py:35
  827.0 18.3 %scatter_fusion = f32[64,6145]{0,1:T(8,128)S(1)} fusion(f32[64,6145]{0,1:T(8,128)S(1)} %get-tuple-element.129, s32[3072]{0:T(1024)S(1)} %bitcast.82, f32[3072,64]{1,0:T(8,128)} %fusion.31), kind=kCustom, calls=%fused_computation.3.clone.1 | custom fusion | flops 196608 | bytes 2371584 | tf_op jit(solution)/shard_map/while/body/eval_jaxpr/scatter-add | solution.py:35
  865.1 18.3 %scatter_fusion = f32[64,6145]{0,1:T(8,128)S(1)} fusion(f32[64,6145]{0,1:T(8,128)S(1)} %get-tuple-element.129, s32[3072]{0:T(1024)S(1)} %bitcast.82, f32[3072,64]{1,0:T(8,128)} %fusion.31), kind=kCustom, calls=%fused_computation.3.clone.1 | custom fusion | flops 196608 | bytes 2371584 | tf_op jit(solution)/shard_map/while/body/eval_jaxpr/scatter-add | solution.py:35
  903.3 18.3 %scatter_fusion = f32[64,6145]{0,1:T(8,128)S(1)} fusion(f32[64,6145]{0,1:T(8,128)S(1)} %get-tuple-element.129, s32[3072]{0:T(1024)S(1)} %bitcast.82, f32[3072,64]{1,0:T(8,128)} %fusion.31), kind=kCustom, calls=%fused_computation.3.clone.1 | custom fusion | flops 196608 | bytes 2371584 | tf_op jit(solution)/shard_map/while/body/eval_jaxpr/scatter-add | solution.py:35
  941.5 18.3 %scatter_fusion = f32[64,6145]{0,1:T(8,128)S(1)} fusion(f32[64,6145]{0,1:T(8,128)S(1)} %get-tuple-element.129, s32[3072]{0:T(1024)S(1)} %bitcast.82, f32[3072,64]{1,0:T(8,128)} %fusion.31), kind=kCustom, calls=%fused_computation.3.clone.1 | custom fusion | flops 196608 | bytes 2371584 | tf_op jit(solution)/shard_map/while/body/eval_jaxpr/scatter-add | solution.py:35
  979.7 18.3 %scatter_fusion = f32[64,6145]{0,1:T(8,128)S(1)} fusion(f32[64,6145]{0,1:T(8,128)S(1)} %get-tuple-element.129, s32[3072]{0:T(1024)S(1)} %bitcast.82, f32[3072,64]{1,0:T(8,128)} %fusion.31), kind=kCustom, calls=%fused_computation.3.clone.1 | custom fusion | flops 196608 | bytes 2371584 | tf_op jit(solution)/shard_map/while/body/eval_jaxpr/scatter-add | solution.py:35
  1017.9 18.3 %scatter_fusion = f32[64,6145]{0,1:T(8,128)S(1)} fusion(f32[64,6145]{0,1:T(8,128)S(1)} %get-tuple-element.129, s32[3072]{0:T(1024)S(1)} %bitcast.82, f32[3072,64]{1,0:T(8,128)} %fusion.31), kind=kCustom, calls=%fused_computation.3.clone.1 | custom fusion | flops 196608 | bytes 2371584 | tf_op jit(solution)/shard_map/while/body/eval_jaxpr/scatter-add | solution.py:35
  1056.1 18.3 %scatter_fusion = f32[64,6145]{0,1:T(8,128)S(1)} fusion(f32[64,6145]{0,1:T(8,128)S(1)} %get-tuple-element.129, s32[3072]{0:T(1024)S(1)} %bitcast.82, f32[3072,64]{1,0:T(8,128)} %fusion.31), kind=kCustom, calls=%fused_computation.3.clone.1 | custom fusion | flops 196608 | bytes 2371584 | tf_op jit(solution)/shard_map/while/body/eval_jaxpr/scatter-add | solution.py:35
  1076.7 43.0 %gather_fusion.2 = f32[12288,64]{1,0:T(8,128)} fusion(f32[64,6145]{0,1:T(8,128)} %concatenate.27, s32[12288]{0:T(1024)S(1)} %copy-done.6), kind=kCustom, calls=%fused_computation.2 | custom fusion | bytes 6340608 | tf_op jit(solution)/shard_map/jit(_take)/gather | solution.py:66
  1157.8 90.2 %all-to-all-start = ((f32[32,1,24576]{2,1,0:T(1,128)}), f32[32,1,24576]{2,1,0:T(1,128)}, u32[]{:S(2)}, u32[]{:S(2)}) async-start(f32[32,1,24576]{2,1,0:T(1,128)} %reshape.246), calls=%async_computation | async-start | bytes 6291456 | tf_op jit(solution)/shard_map/all_to_all | solution.py:67
  1253.4 66.3 %all-to-all-done = f32[32,1,24576]{2,1,0:T(1,128)} async-done(((f32[32,1,24576]{2,1,0:T(1,128)}), f32[32,1,24576]{2,1,0:T(1,128)}, u32[]{:S(2)}, u32[]{:S(2)}) %all-to-all-start) | async-done | bytes 3145760 | tf_op jit(solution)/shard_map/all_to_all | solution.py:67
  1346.4 66.4 %scatter_custom_fusion.1 = f32[128,3073]{0,1:T(8,128)S(1)} fusion(s32[12288]{0:T(1024)S(1)} %bitcast.85, f32[12288,128]{1,0:T(8,128)} %bitcast.79, f32[]{:T(128)} %constant.47.clone.1), kind=kCustom, calls=%fused_computation.34 | custom fusion | flops 1572864 | bytes 1573888 | tf_op jit(solution)/shard_map/scatter-add | solution.py:72
  (214 shorter events, 654.0 us)
Async XLA Ops:
  0.6 1334.1 %copy-start = (f32[8,128,64]{1,2,0:T(8,128)S(1)}, f32[8,128,64]{1,2,0:T(8,128)}, u32[]{:S(2)}) copy-start(f32[8,128,64]{1,2,0:T(8,128)} %param.23) | copy-start | bytes 786436
  0.6 2.2 copy-start.9
  2.8 22.2 %copy-start.1 = (f32[1,1,1,64,6144]{3,4,2,1,0:T(8,128)}, f32[1,1,1,64,6144]{3,4,2,1,0:T(8,128)S(1)}, u32[]{:S(2)}) copy-start(f32[1,1,1,64,6144]{3,4,2,1,0:T(8,128)S(1)} %copy.34) | copy-start | bytes 4718596
  6.4 9.7 collective-permute-start
  10.9 10.0 collective-permute-start.1
  25.0 15.0 %collective-permute-start.2 = (f32[64,3,1,1,512]{4,0,3,2,1:T(8,128)}, f32[64,3,1,1,512]{4,0,3,2,1:T(8,128)}, u32[]{:S(2)}, u32[]{:S(2)}) collective-permute-start(f32[64,3,1,1,512]{4,0,3,2,1:T(8,128)} %copy.35), channel_id=1, source_target_pairs={{0,2},{2,4},{4,6},{1,3},{3,5},{5,7},{8,10},{10,12},{12,14},{9,11},... | collective-permute-start | bytes 1179656 | tf_op jit(solution)/shard_map/ppermute | solution.py:17
  28.5 12.8 collective-permute-start.3
  41.3 4.4 copy-start.3
  45.8 9.7 collective-permute-start.4
  48.1 10.3 collective-permute-start.5
  51.7 2.8 copy-start.4
  51.7 2.8 copy-start.5
  61.2 4.0 copy-start.2
  81.6 992.8 %copy-start.10 = (f32[64]{0:T(128)S(1)}, f32[64]{0:T(128)}, u32[]{:S(2)}) copy-start(f32[64]{0:T(128)} %param.22) | copy-start | bytes 772
  81.6 992.8 %copy-start.11 = (f32[64]{0:T(128)S(1)}, f32[64]{0:T(128)}, u32[]{:S(2)}) copy-start(f32[64]{0:T(128)} %param.21) | copy-start | bytes 772
  1074.7 1.9 copy-start.6
  1126.2 7.3 copy-start.7
  1157.8 90.3 %copy-start.8 = (s32[1,1,1,32,384]{4,3,2,1,0:T(8,128)S(1)}, s32[1,1,1,32,384]{4,3,2,1,0:T(8,128)}, u32[]{:S(2)}) copy-start(s32[1,1,1,32,384]{4,3,2,1,0:T(8,128)} %param.19) | copy-start | bytes 147460
  1157.8 161.9 %all-to-all-start = ((f32[32,1,24576]{2,1,0:T(1,128)}), f32[32,1,24576]{2,1,0:T(1,128)}, u32[]{:S(2)}, u32[]{:S(2)}) async-start(f32[32,1,24576]{2,1,0:T(1,128)} %reshape.246), calls=%async_computation | async-start | bytes 6291456 | tf_op jit(solution)/shard_map/all_to_all | solution.py:67
  1342.8 69.9 %copy-start.12 = (f32[128]{0:T(128)S(1)}, f32[128]{0:T(128)}, u32[]{:S(2)}) copy-start(f32[128]{0:T(128)} %param.25) | copy-start | bytes 1540
  1342.8 69.9 %copy-start.13 = (f32[128]{0:T(128)S(1)}, f32[128]{0:T(128)}, u32[]{:S(2)}) copy-start(f32[128]{0:T(128)} %param.24) | copy-start | bytes 1540
where the time goes:
time: 1420 us; the launch traced here: 1410 us
  other arithmetic  619 us (44%)
  local copies, waits for them, and re-layouts  496 us (35%)
  matrix products  120 us (8%)
  starting transfers between devices  106 us (7%)
  waiting for transfers between devices  71.3 us (5%)
    scatter-add x26, other arithmetic, step(): acc.at[:, dst_cols].add(jnp.dot(weight, picked, precision=HIGH))  476 us
    gather x26, local copies, waits for them, and re-layouts, step(): picked = jnp.take(source, src_cols, axis=1)  385 us
    dot_general x26, matrix products, step(): jnp.dot(weight, picked, precision=HIGH)  104 us
    all_to_all x1, starting transfers between devices, body(): lax.all_to_all(packed, 'gx', split_axis=1, concat_axis=1, tiled=True)  90.2 us
    scatter-add x1, other arithmetic, body(): total = jnp.zeros((outputs, COARSE + 1), jnp.float32).at[:, cols].add(flat)  66.4 us
    all_to_all x1, waiting for transfers between devices, body(): lax.all_to_all(packed, 'gx', split_axis=1, concat_axis=1, tiled=True)  66.3 us
    gather x3, local copies, waits for them, and re-layouts, body(): jnp.take(fine_pad, table, axis=1).reshape(chans, owners, 8, slots // 8)  56.9 us
  transfers between devices with their start and end apart: 7, of which 3 were waited for; matrix products, arithmetic and copies ran while one was open for 2% of the time, Pallas kernels for 0%

commit v1 on v0

v1 whole, which is shorter than its diff:
```python
import functools

import jax
import jax.numpy as jnp
from jax import lax
from jax.experimental import pallas as pl
from jax.experimental.pallas import tpu as pltpu
from jax.sharding import PartitionSpec as P

CH = 64
CHO = 128
VOX = 6144
PAIRS = 3072
BND = 512
COARSE = 3072
OWNERS = 32
CAP = 384
ZERO_ROW = VOX + 27 * BND
TABLE = ZERO_ROW + 8
ROWS = VOX + 8
TILE = 256
TILES = VOX // TILE
PER_TILE = PAIRS // TILES
STEPS = 13
GROUP = 48
HALF = CAP // 2
ACCS = 8
F32 = jnp.float32
BF16 = jnp.bfloat16
MIB = 1 << 20

VMEM = pl.BlockSpec(memory_space=pltpu.VMEM)
SMEM = pl.BlockSpec(memory_space=pltpu.SMEM)
ANY = pl.BlockSpec(memory_space=pl.ANY)


def params(mib):
    return pltpu.CompilerParams(vmem_limit_bytes=mib * MIB)


def low_lanes(rows=1):
    return lax.broadcasted_iota(jnp.int32, (rows, 128), 1) < CH


def split(x):
    hi = x.astype(BF16)
    lo = (x - hi.astype(F32)).astype(BF16)
    return hi, lo


def prep_kernel(own_ref, rows_ref, table_ref, buf_ref):
    def turn(t, carry):
        at = pl.ds(pl.multiple_of(t * TILE, TILE), TILE)
        x = own_ref[:, at]
        table_ref[at, :] = jnp.concatenate([x, x], axis=0).T
        return carry

    lax.fori_loop(0, TILES, turn, 0)
    low = low_lanes()

    def pick(i, carry):
        for u in range(32):
            r = i * 32 + u
            first = table_ref[pl.ds(rows_ref[0, r], 1), :]
            second = table_ref[pl.ds(rows_ref[0, r + BND // 2], 1), :]
            buf_ref[pl.ds(r, 1), :] = jnp.where(low, first, second)
        return carry

    lax.fori_loop(0, BND // 64, pick, 0)


def prep(own, rows):
    return pl.pallas_call(
        prep_kernel,
        out_shape=(
            jax.ShapeDtypeStruct((VOX, 128), F32),
            jax.ShapeDtypeStruct((BND // 2, 128), F32),
        ),
        in_specs=[VMEM, SMEM],
        out_specs=(VMEM, VMEM),
        compiler_params=params(32),
        name="prep",
    )(own, rows)


def spread(s_ref, start, buf):
    other = pltpu.roll(buf, CH, 1)
    low = low_lanes(BND // 2)
    s_ref[pl.ds(start, BND // 2), :] = jnp.where(low, buf, other)
    s_ref[pl.ds(start + BND // 2, BND // 2), :] = jnp.where(low, other, buf)


def conv_kernel(
    place_ref, own_ref, mid_ref, far_ref, ins_ref, outs_ref, w_ref, scale_ref, shift_ref,
    fine_ref, rows_ref,
    s_ref, g0_ref, g1_ref, acc_ref, in_ref, out_ref, own_sem, cen_sem, in_sem, out_sem,
):
    own_copy = pltpu.make_async_copy(own_ref, s_ref.at[pl.ds(0, VOX), :], own_sem)
    cen_copy = pltpu.make_async_copy(own_ref, g1_ref.at[pl.ds(0, VOX), :], cen_sem)
    own_copy.start()
    cen_copy.start()

    def lists(s, slot):
        return (
            pltpu.make_async_copy(ins_ref.at[pl.ds(2 * s, 2)], in_ref.at[slot], in_sem.at[slot]),
            pltpu.make_async_copy(outs_ref.at[pl.ds(2 * s, 2)], out_ref.at[slot], out_sem.at[slot]),
        )

    for copy in lists(0, 0):
        copy.start()
    here = place_ref[0]
    other = 2 - 2 * here
    same = 2 * here
    empty = jnp.zeros((BND, 128), F32)

    def fill(e, carry):
        base = VOX + e * 3 * BND
        spread(s_ref, pl.multiple_of(base + BND, BND), mid_ref[e])
        spread(s_ref, pl.multiple_of(base + other * BND, BND), far_ref[e])
        s_ref[pl.ds(pl.multiple_of(base + same * BND, BND), BND), :] = empty
        return carry

    lax.fori_loop(0, 9, fill, 0)
    s_ref[pl.ds(ZERO_ROW, 8), :] = jnp.zeros((8, 128), F32)

    def clear(t, carry):
        at = pl.ds(pl.multiple_of(t * TILE, TILE), TILE)
        g0_ref[at, :] = jnp.zeros((TILE, 128), F32)
        acc_ref[at, :] = jnp.zeros((TILE, 128), F32)
        return carry

    lax.fori_loop(0, TILES, clear, 0)
    low = low_lanes()
    high = jnp.logical_not(low)
    own_copy.wait()
    cen_copy.wait()

    def product(ref, at, s):
        hi, lo = split(ref[at, :])
        return jnp.dot(
            jnp.concatenate([hi, lo], axis=1), w_ref[s], preferred_element_type=F32
        )

    def phase(s, slot, now_ref, last_ref, more):
        for copy in lists(s, slot):
            copy.wait()
        if more:
            for copy in lists(s + 1, 1 - slot):
                copy.start()

        def body(t, carry):
            at = pl.ds(pl.multiple_of(t * TILE, TILE), TILE)
            acc_ref[at, :] += product(last_ref, at, s)
            last_ref[at, :] = jnp.zeros((TILE, 128), F32)
            for u in range(PER_TILE):
                p = t * PER_TILE + u
                for j, mask in ((0, low), (1, high)):
                    row = s_ref[pl.ds(in_ref[slot, j, 0, p], 1), :]
                    pltpu.store(
                        now_ref.at[pl.ds(out_ref[slot, j, 0, p], 1), :], row, mask=mask
                    )
            return carry

        lax.fori_loop(0, TILES, body, 0)

    def two(i, carry):
        phase(2 * i, 0, g0_ref, g1_ref, True)
        phase(2 * i + 1, 1, g1_ref, g0_ref, True)
        return carry

    lax.fori_loop(0, (STEPS - 1) // 2, two, 0)
    phase(STEPS - 1, 0, g0_ref, g1_ref, False)
    low_tile = low_lanes(128)

    def finish(t, carry):
        at = pl.ds(pl.multiple_of(t * TILE, TILE), TILE)
        total = acc_ref[at, :] + product(g0_ref, at, STEPS)
        total = total + pltpu.roll(total, CH, 1)
        fine = jnp.maximum(scale_ref[...] * total + shift_ref[...], 0.0)
        rows_ref[at, :] = fine
        turned = jnp.where(low_tile, fine[:128], fine[128:]).T
        fine_ref[:, pl.ds(pl.multiple_of(t * TILE, TILE), 128)] = turned[:CH]
        fine_ref[:, pl.ds(pl.multiple_of(t * TILE + 128, 128), 128)] = turned[CH:]
        return carry

    lax.fori_loop(0, TILES, finish, 0)
    rows_ref[pl.ds(VOX, 8), :] = jnp.zeros((8, 128), F32)


def conv(place, own, mid, far, ins, outs, weights, scale, shift):
    return pl.pallas_call(
        conv_kernel,
        out_shape=(
            jax.ShapeDtypeStruct((CH, VOX), F32),
            jax.ShapeDtypeStruct((ROWS, 128), F32),
        ),
        in_specs=[SMEM, ANY, VMEM, VMEM, ANY, ANY, VMEM, VMEM, VMEM],
        out_specs=(VMEM, VMEM),
        scratch_shapes=[
            pltpu.VMEM((TABLE, 128), F32),
            pltpu.VMEM((ROWS, 128), F32),
            pltpu.VMEM((ROWS, 128), F32),
            pltpu.VMEM((VOX, 128), F32),
            pltpu.SMEM((2, 2, 1, PAIRS), jnp.int32),
            pltpu.SMEM((2, 2, 1, PAIRS), jnp.int32),
            pltpu.SemaphoreType.DMA,
            pltpu.SemaphoreType.DMA,
            pltpu.SemaphoreType.DMA((2,)),
            pltpu.SemaphoreType.DMA((2,)),
        ],
        compiler_params=params(48),
        name="conv",
    )(place, own, mid, far, ins, outs, weights, scale, shift)


def pack_kernel(rows_ref, table_ref, out_ref):
    low = low_lanes()

    def owner(a, carry):
        for r in range(HALF):
            first = rows_ref[pl.ds(table_ref[a, r], 1), :]
            second = rows_ref[pl.ds(table_ref[a, r + HALF], 1), :]
            out_ref[a, pl.ds(r, 1), :] = jnp.where(low, first, second)
        return carry

    lax.fori_loop(0, OWNERS, owner, 0)


def pack(rows, table):
    return pl.pallas_call(
        pack_kernel,
        out_shape=jax.ShapeDtypeStruct((OWNERS, HALF, 128), F32),
        in_specs=[VMEM, SMEM],
        out_specs=VMEM,
        compiler_params=params(32),
        name="pack",
    )(rows, table)


def down_kernel(x_ref, cols_ref, w_ref, scale_ref, shift_ref, out_ref, p0_ref, p1_ref, *z_refs):
    def clear(t, carry):
        at = pl.ds(pl.multiple_of(t * 128, 128), 128)
        for z_ref in z_refs:
            z_ref[at, :] = jnp.zeros((128, 128), F32)
        return carry

    lax.fori_loop(0, COARSE // 128, clear, 0)

    def source(s, carry):
        for c in range(4):
            hi, lo = split(x_ref[s, pl.ds(c * GROUP, GROUP), :])
            part = jnp.dot(hi, w_ref[0, c], preferred_element_type=F32)
            part += jnp.dot(lo, w_ref[0, c], preferred_element_type=F32)
            part += jnp.dot(hi, w_ref[1, c], preferred_element_type=F32)
            p0_ref[pl.ds(c * GROUP, GROUP), :] = part[:, :128]
            p1_ref[pl.ds(c * GROUP, GROUP), :] = part[:, 128:]
        for r in range(0, HALF, ACCS // 2):
            todo = []
            for u in range(ACCS // 2):
                for j, p_ref in enumerate((p0_ref, p1_ref)):
                    at = pl.ds(cols_ref[s, r + u + j * HALF], 1)
                    z_ref = z_refs[2 * u + j]
                    todo.append((z_ref, at, z_ref[at, :] + p_ref[pl.ds(r + u, 1), :]))
            for z_ref, at, value in todo:
                z_ref[at, :] = value
        return carry

    lax.fori_loop(0, OWNERS, source, 0)

    def finish(t, carry):
        at = pl.ds(pl.multiple_of(t * 128, 128), 128)
        total = z_refs[0][at, :]
        for z_ref in z_refs[1:]:
            total = total + z_ref[at, :]
        out_ref[:, at] = jnp.maximum(scale_ref[...] * total + shift_ref[...], 0.0).T
        return carry

    lax.fori_loop(0, COARSE // 128, finish, 0)


def down(arrived, cols, weights, scale, shift):
    return pl.pallas_call(
        down_kernel,
        out_shape=jax.ShapeDtypeStruct((CHO, COARSE), F32),
        in_specs=[VMEM, SMEM, VMEM, VMEM, VMEM],
        out_specs=VMEM,
        scratch_shapes=[pltpu.VMEM((HALF, 128), F32)] * 2
        + [pltpu.VMEM((COARSE + 8, 128), F32)] * ACCS,
        compiler_params=params(48),
        name="down",
    )(arrived, cols, weights, scale, shift)


def neighbours(axis, block):
    count = lax.axis_size(axis)
    forward = [(i, i + 1) for i in range(count - 1)]
    backward = [(target, source) for source, target in forward]
    return lax.ppermute(block, axis, forward), lax.ppermute(block, axis, backward)


def two_parts(w):
    hi = lax.reduce_precision(w, 8, 7)
    return hi.astype(BF16), (w - hi).astype(BF16)


def conv_weights(w):
    hi, lo = two_parts(jnp.swapaxes(w, 1, 2))
    top = jnp.concatenate([hi, lo], axis=2)
    bottom = jnp.concatenate([hi, jnp.zeros_like(hi)], axis=2)

    def arrange(x):
        pairs = jnp.concatenate([x[:13], x[14:]], axis=0).reshape(STEPS, 128, 128)
        centre = jnp.concatenate([x[13], jnp.zeros_like(x[13])], axis=0)
        return jnp.concatenate([centre[None], pairs], axis=0)

    return jnp.concatenate([arrange(top), arrange(bottom)], axis=1)


def down_weights(w):
    turned = jnp.swapaxes(w, 1, 2)
    zero = jnp.zeros_like(turned[:4])
    both = jnp.concatenate(
        [
            jnp.concatenate([turned[:4], zero], axis=2),
            jnp.concatenate([zero, turned[4:]], axis=2),
        ],
        axis=1,
    )
    return jnp.stack(two_parts(both))


def body(
    features,
    boundary_rows,
    in_maps,
    out_maps,
    send_rows,
    recv_coarse,
    conv_weight,
    scale_one,
    shift_one,
    down_weight,
    scale_two,
    shift_two,
):
    own, buf = prep(features[0, 0, 0], boundary_rows[0, 0])
    left, right = neighbours("gx", buf)
    line = jnp.stack([left, buf, right])
    low, high = neighbours("gy", line)
    mid = jnp.stack([low, line, high], axis=1).reshape(9, BND // 2, 128)
    far = lax.ppermute(mid, "gz", [(0, 1), (1, 0)])
    place = lax.axis_index("gz").astype(jnp.int32).reshape(1)
    fine, rows = conv(
        place,
        own,
        mid,
        far,
        in_maps[0, 0, 0].reshape(26, 1, PAIRS),
        out_maps[0, 0, 0].reshape(26, 1, PAIRS),
        conv_weights(conv_weight),
        jnp.tile(scale_one, 2)[None],
        jnp.tile(shift_one, 2)[None],
    )
    packed = pack(rows, send_rows[0, 0, 0])
    arrived = lax.all_to_all(packed, "gx", split_axis=0, concat_axis=0, tiled=True)
    coarse = down(
        arrived,
        recv_coarse[0, 0, 0],
        down_weights(down_weight),
        scale_two[None],
        shift_two[None],
    )
    return (fine[None, None, None], coarse[None, None, None])


def solution(mesh):
    return jax.shard_map(
        body,
        mesh=mesh,
        in_specs=(
            P("gx", "gy", "gz", None, None),
            P("gx", "gy", "gz", None),
            P("gx", "gy", "gz", None, None),
            P("gx", "gy", "gz", None, None),
            P("gx", "gy", "gz", None, None),
            P("gx", "gy", "gz", None, None),
            P(),
            P(),
            P(),
            P(),
            P(),
            P(),
        ),
        out_specs=(P("gx", "gy", "gz", None, None), P("gx", "gy", "gz", None, None)),
        check_vma=False,
    )
```

time: 1420 us -> 348 us (0.25)
  other arithmetic: 619 us -> 1.71 us
  local copies, waits for them, and re-layouts: 496 us -> 8.92 us
  Pallas kernels: 0 us -> 225 us
  matrix products: 120 us -> 0 us
  starting transfers between devices: 106 us -> 21.8 us
  waiting for transfers between devices: 71.3 us -> 87.1 us
    scatter-add x27 -> x0, other arithmetic: 543 us -> none  [the longest x26 476 us: step(): acc.at[:, dst_cols].add(jnp.dot(weight, picked, precision=HIGH))]
    gather x30 -> x0, local copies, waits for them, and re-layouts: 444 us -> none  [the longest x26 385 us: step(): picked = jnp.take(source, src_cols, axis=1)]
    pallas_call x0 -> x4, Pallas kernels: none -> 225 us  [the longest x1 178 us: conv(): pl.pallas_call(conv_kernel, out_shape=(jax.ShapeDtypeStruct((CH, VOX), F3...]
    dot_general x27 -> x0, matrix products: 112 us -> none  [the longest x26 104 us: step(): jnp.dot(weight, picked, precision=HIGH)]
    all_to_all x1, starting transfers between devices: 90.2 us -> 10.8 us  [body(): lax.all_to_all(packed, 'gx', split_axis=0, concat_axis=0, tiled=True)]
    select_n x31 -> x0, other arithmetic: 36.1 us -> none  [the longest x26 25.6 us: step(): picked = jnp.take(source, src_cols, axis=1)]
    concatenate x5 -> x3, other arithmetic: 25.7 us -> 0.34 us  [the longest x2 0.28 us: arrange(): pairs = jnp.concatenate([x[:13], x[14:]], axis=0).reshape(STEPS, 128, 128)]
  transfers between devices with their start and end apart: 7 -> 6, of which waited for: 3 -> 6; matrix products, arithmetic and copies ran while one was open for 2% -> 1% of each run, Pallas kernels for 0% -> 0%
where the time goes in v1:
time: 348 us; the launch traced here: 345 us
  Pallas kernels  225 us (65%)
  waiting for transfers between devices  87.1 us (25%)
  starting transfers between devices  21.8 us (6%)
  local copies, waits for them, and re-layouts  8.92 us (3%)
    pallas_call x1, Pallas kernels, conv(): pl.pallas_call(conv_kernel, out_shape=(jax.ShapeDtypeStruct((CH, VOX), F3...  178 us
    all_to_all x1, waiting for transfers between devices, body(): lax.all_to_all(packed, 'gx', split_axis=0, concat_axis=0, tiled=True)  72 us
    pallas_call x1, Pallas kernels, down(): pl.pallas_call(down_kernel, out_shape=jax.ShapeDtypeStruct((CHO, COARSE),...  28 us
    pallas_call x1, Pallas kernels, pack(): pl.pallas_call(pack_kernel, out_shape=jax.ShapeDtypeStruct((OWNERS, HALF,...  15.4 us
    all_to_all x1, starting transfers between devices, body(): lax.all_to_all(packed, 'gx', split_axis=0, concat_axis=0, tiled=True)  10.8 us
    unnamed x31, local copies, waits for them, and re-layouts  8.5 us
    ppermute x2, waiting for transfers between devices, neighbours(): lax.ppermute(block, axis, backward)  7.51 us
    ppermute x2, starting transfers between devices, neighbours(): lax.ppermute(block, axis, forward)  7.31 us
  transfers between devices with their start and end apart: 6, of which 6 were waited for; matrix products, arithmetic and copies ran while one was open for 1% of the time, Pallas kernels for 0%

profile of v1, /device:TPU:8, one launch (start us, length us, event | category | flops | bytes accessed | tf_op | source)
XLA Modules:
  0.0 345.1 jit_solution(10414279052872419641)
XLA Ops:
  0.6 1.4 copy-done.4
  2.0 0.7 copy-done.9
  2.7 3.4 prep.1
  6.1 3.8 %collective-permute-start = (f32[256,128]{1,0:T(8,128)S(1)}, f32[256,128]{1,0:T(8,128)S(1)}, u32[]{:S(2)}, u32[]{:S(2)}) collective-permute-start(f32[256,128]{1,0:T(8,128)S(1)} %get-tuple-element.7), channel_id=1, source_target_pairs={{0,8},{8,16},{16,24},{24,32},{32,40},{40,48},{48,56},{56,64},{64,7... | collective-permute-start | bytes 393224 | tf_op jit(solution)/shard_map/ppermute | solution.py:298
  10.0 1.3 collective-permute-start.1
  11.3 1.4 collective-permute-done
  12.7 4.3 %collective-permute-done.1 = f32[256,128]{1,0:T(8,128)S(1)} collective-permute-done((f32[256,128]{1,0:T(8,128)S(1)}, f32[256,128]{1,0:T(8,128)S(1)}, u32[]{:S(2)}, u32[]{:S(2)}) %collective-permute-start.1) | collective-permute-done | bytes 131104 | tf_op jit(solution)/shard_map/ppermute | solution.py:298
  17.1 3.5 %collective-permute-start.2 = (f32[3,256,128]{2,1,0:T(8,128)S(1)}, f32[3,256,128]{2,1,0:T(8,128)S(1)}, u32[]{:S(2)}, u32[]{:S(2)}) collective-permute-start(f32[3,256,128]{2,1,0:T(8,128)S(1)} %get-tuple-element.19), channel_id=1, source_target_pairs={{0,2},{2,4},{4,6},{1,3},{3,5},{5,7},{8,10},{10,12},{12,14},{9,11},... | collective-permute-start | bytes 1179656 | tf_op jit(solution)/shard_map/ppermute | solution.py:298
  20.6 2.4 collective-permute-start.3
  22.9 5.9 %collective-permute-done.2 = f32[3,256,128]{2,1,0:T(8,128)S(1)} collective-permute-done((f32[3,256,128]{2,1,0:T(8,128)S(1)}, f32[3,256,128]{2,1,0:T(8,128)S(1)}, u32[]{:S(2)}, u32[]{:S(2)}) %collective-permute-start.2) | collective-permute-done | bytes 393248 | tf_op jit(solution)/shard_map/ppermute | solution.py:298
  28.8 3.2 collective-permute-done.3
  32.2 0.1 collective-permute-start.4
  32.3 1.5 copy.15
  33.8 0.1 broadcast_in_dim_tile.6.scale_ref
  33.9 0.1 broadcast_in_dim_tile.7.shift_ref
  34.0 0.2 fusion
  34.2 0.1 maximum_bitcast_fusion
  34.3 0.1 pad_slice_fusion.1
  34.5 0.2 fusion.7
  34.8 0.3 collective-permute-done.4.far_ref
  35.2 0.2 copy-done.5
  35.4 0.1 copy-done.6
  35.5 177.7 %conv.1 = (f32[64,6144]{1,0:T(8,128)}, f32[6152,128]{1,0:T(8,128)}) custom-call(s32[1]{0:T(128)} %bitcast.place_ref, f32[6144,128]{1,0:T(8,128)} %copy-done.2, f32[9,256,128]{2,1,0:T(8,128)S(1)} %bitcast.38, f32[9,256,128]{2,1,0:T(8,128)S(1)} %collective-permute-done.4.far_ref, s32[26,1,3072]{2,1,0:T(1,128)S(1)} %bitcast.40, s32[26,1,3072]{2,1,0:T(1,128)S(1)} %bitcast.41, ...), custom_call_target="tpu_custom_call" | custom-call | tf_op jit(solution)/shard_map/conv/pallas_call | solution.py:191
  213.3 1.9 copy-done.1
  215.2 15.4 %pack.1 = f32[32,192,128]{2,1,0:T(8,128)S(1)} custom-call(f32[6152,128]{1,0:T(8,128)S(1)} %copy-done.1, s32[32,384]{1,0:T(8,128)S(1)} %bitcast.43), custom_call_target="tpu_custom_call" | custom-call | tf_op jit(solution)/shard_map/pack/pallas_call | solution.py:230
  230.6 1.6 copy-done
  232.2 10.8 %all-to-all-start = ((f32[32,192,128]{2,1,0:T(8,128)}), f32[32,192,128]{2,1,0:T(8,128)S(1)}, u32[]{:S(2)}, u32[]{:S(2)}) async-start(f32[32,192,128]{2,1,0:T(8,128)} %copy-done), calls=%async_computation | async-start | bytes 6291456 | tf_op jit(solution)/shard_map/all_to_all | solution.py:365
  243.1 0.1 reduce-precision_convert_fusion.1
  243.2 0.8 pad_maximum_fusion.2.w_ref
  244.1 72.0 %all-to-all-done.x_ref = f32[32,192,128]{2,1,0:T(8,128)S(1)} async-done(((f32[32,192,128]{2,1,0:T(8,128)}), f32[32,192,128]{2,1,0:T(8,128)S(1)}, u32[]{:S(2)}, u32[]{:S(2)}) %all-to-all-start) | async-done | bytes 3145760 | tf_op jit(solution)/shard_map/all_to_all | solution.py:365
  316.1 1.0 copy-done.3
  317.1 28.0 %down.1 = f32[128,3072]{1,0:T(8,128)} custom-call(f32[32,192,128]{2,1,0:T(8,128)S(1)} %all-to-all-done.x_ref, s32[32,384]{1,0:T(8,128)S(1)} %bitcast.44, bf16[2,4,128,256]{3,2,1,0:T(8,128)(2,1)S(1)} %copy-done.3, f32[1,128]{1,0:T(1,128)S(1)} %bitcast.46, f32[1,128]{1,0:T(1,128)S(1)} %bitcast.47), custom_call_target="tpu_custom_call" | custom-call | tf_op jit(solution)/shard_map/down/pallas_call | solution.py:282
  (33 shorter events, 0.4 us)
Async XLA Ops:
  0.6 1.4 copy-start.4
  2.0 0.7 copy-start.9
  6.1 26.1 %copy-start.2 = (f32[6144,128]{1,0:T(8,128)}, f32[6144,128]{1,0:T(8,128)S(1)}, u32[]{:S(2)}) copy-start(f32[6144,128]{1,0:T(8,128)S(1)} %get-tuple-element.6.own_ref) | copy-start | bytes 9437188
  6.1 6.6 %collective-permute-start = (f32[256,128]{1,0:T(8,128)S(1)}, f32[256,128]{1,0:T(8,128)S(1)}, u32[]{:S(2)}, u32[]{:S(2)}) collective-permute-start(f32[256,128]{1,0:T(8,128)S(1)} %get-tuple-element.7), channel_id=1, source_target_pairs={{0,8},{8,16},{16,24},{24,32},{32,40},{40,48},{48,56},{56,64},{64,7... | collective-permute-start | bytes 393224 | tf_op jit(solution)/shard_map/ppermute | solution.py:298
  10.0 7.0 %collective-permute-start.1 = (f32[256,128]{1,0:T(8,128)S(1)}, f32[256,128]{1,0:T(8,128)S(1)}, u32[]{:S(2)}, u32[]{:S(2)}) collective-permute-start(f32[256,128]{1,0:T(8,128)S(1)} %get-tuple-element.7), channel_id=1, source_target_pairs={{8,0},{16,8},{24,16},{32,24},{40,32},{48,40},{56,48},{64,56},{72,6... | collective-permute-start | bytes 393224 | tf_op jit(solution)/shard_map/ppermute | solution.py:298
  17.1 11.8 %collective-permute-start.2 = (f32[3,256,128]{2,1,0:T(8,128)S(1)}, f32[3,256,128]{2,1,0:T(8,128)S(1)}, u32[]{:S(2)}, u32[]{:S(2)}) collective-permute-start(f32[3,256,128]{2,1,0:T(8,128)S(1)} %get-tuple-element.19), channel_id=1, source_target_pairs={{0,2},{2,4},{4,6},{1,3},{3,5},{5,7},{8,10},{10,12},{12,14},{9,11},... | collective-permute-start | bytes 1179656 | tf_op jit(solution)/shard_map/ppermute | solution.py:298
  20.6 11.5 %collective-permute-start.3 = (f32[3,256,128]{2,1,0:T(8,128)S(1)}, f32[3,256,128]{2,1,0:T(8,128)S(1)}, u32[]{:S(2)}, u32[]{:S(2)}) collective-permute-start(f32[3,256,128]{2,1,0:T(8,128)S(1)} %get-tuple-element.19), channel_id=1, source_target_pairs={{2,0},{4,2},{6,4},{3,1},{5,3},{7,5},{10,8},{12,10},{14,12},{11,9},... | collective-permute-start | bytes 1179656 | tf_op jit(solution)/shard_map/ppermute | solution.py:298
  32.1 1.7 copy-start.13
  32.1 1.8 copy-start.14
  32.2 2.9 collective-permute-start.4
  34.4 1.0 copy-start.5
  34.5 1.1 copy-start.6
  35.5 177.8 %copy-start.7 = (s32[1,1,1,32,384]{4,3,2,1,0:T(8,128)S(1)}, s32[1,1,1,32,384]{4,3,2,1,0:T(8,128)}, u32[]{:S(2)}) copy-start(s32[1,1,1,32,384]{4,3,2,1,0:T(8,128)} %param.16) | copy-start | bytes 147460
  213.3 1.9 copy-start.1
  230.6 1.6 copy-start
  232.2 10.8 %copy-start.12 = (f32[8,128,64]{1,2,0:T(8,128)S(1)}, f32[8,128,64]{1,2,0:T(8,128)}, u32[]{:S(2)}) copy-start(f32[8,128,64]{1,2,0:T(8,128)} %param.21) | copy-start | bytes 786436
  232.2 83.8 %all-to-all-start = ((f32[32,192,128]{2,1,0:T(8,128)}), f32[32,192,128]{2,1,0:T(8,128)S(1)}, u32[]{:S(2)}, u32[]{:S(2)}) async-start(f32[32,192,128]{2,1,0:T(8,128)} %copy-done), calls=%async_computation | async-start | bytes 6291456 | tf_op jit(solution)/shard_map/all_to_all | solution.py:365
  243.0 73.0 %copy-start.8 = (s32[1,1,1,32,384]{4,3,2,1,0:T(8,128)S(1)}, s32[1,1,1,32,384]{4,3,2,1,0:T(8,128)}, u32[]{:S(2)}) copy-start(s32[1,1,1,32,384]{4,3,2,1,0:T(8,128)} %param.17) | copy-start | bytes 147460
  243.0 73.0 %copy-start.10 = (f32[128]{0:T(128)S(1)}, f32[128]{0:T(128)}, u32[]{:S(2)}) copy-start(f32[128]{0:T(128)} %param.22) | copy-start | bytes 1540
  243.0 73.0 %copy-start.11 = (f32[128]{0:T(128)S(1)}, f32[128]{0:T(128)}, u32[]{:S(2)}) copy-start(f32[128]{0:T(128)} %param.23) | copy-start | bytes 1540
  316.1 1.0 copy-start.3

commit v2 on v1

--- a/solution.py
+++ b/solution.py
@@ -20,11 +20,15 @@
 ROWS = VOX + 8
 TILE = 256
 TILES = VOX // TILE
-PER_TILE = PAIRS // TILES
+BLOCK = 512
+BLOCKS = VOX // BLOCK
 STEPS = 13
 GROUP = 48
 HALF = CAP // 2
 ACCS = 8
+CHUNKS = 2
+PART = HALF // CHUNKS
+GROUPS = PART // GROUP
 F32 = jnp.float32
 BF16 = jnp.bfloat16
 MIB = 1 << 20
@@ -93,7 +97,7 @@
 def conv_kernel(
     place_ref, own_ref, mid_ref, far_ref, ins_ref, outs_ref, w_ref, scale_ref, shift_ref,
     fine_ref, rows_ref,
-    s_ref, g0_ref, g1_ref, acc_ref, in_ref, out_ref, own_sem, cen_sem, in_sem, out_sem,
+    s_ref, g0_ref, g1_ref, acc_ref, own_sem, cen_sem, list_sem, *list_refs,
 ):
     own_copy = pltpu.make_async_copy(own_ref, s_ref.at[pl.ds(0, VOX), :], own_sem)
     cen_copy = pltpu.make_async_copy(own_ref, g1_ref.at[pl.ds(0, VOX), :], cen_sem)
@@ -101,10 +105,14 @@
     cen_copy.start()
 
     def lists(s, slot):
-        return (
-            pltpu.make_async_copy(ins_ref.at[pl.ds(2 * s, 2)], in_ref.at[slot], in_sem.at[slot]),
-            pltpu.make_async_copy(outs_ref.at[pl.ds(2 * s, 2)], out_ref.at[slot], out_sem.at[slot]),
-        )
+        return [
+            pltpu.make_async_copy(
+                (ins_ref, outs_ref)[i // 4].at[s, i // 2 % 2, i % 2],
+                ref.at[slot],
+                list_sem.at[slot, i],
+            )
+            for i, ref in enumerate(list_refs)
+        ]
 
     for copy in lists(0, 0):
         copy.start()
@@ -149,19 +157,20 @@
                 copy.start()
 
         def body(t, carry):
-            at = pl.ds(pl.multiple_of(t * TILE, TILE), TILE)
+            at = pl.ds(pl.multiple_of(t * BLOCK, BLOCK), BLOCK)
             acc_ref[at, :] += product(last_ref, at, s)
-            last_ref[at, :] = jnp.zeros((TILE, 128), F32)
-            for u in range(PER_TILE):
-                p = t * PER_TILE + u
-                for j, mask in ((0, low), (1, high)):
-                    row = s_ref[pl.ds(in_ref[slot, j, 0, p], 1), :]
+            last_ref[at, :] = jnp.zeros((BLOCK, 128), F32)
+            for u in range(128):
+                for i in range(4):
+                    row = s_ref[pl.ds(list_refs[i][slot, t, u], 1), :]
                     pltpu.store(
-                        now_ref.at[pl.ds(out_ref[slot, j, 0, p], 1), :], row, mask=mask
+                        now_ref.at[pl.ds(list_refs[i + 4][slot, t, u], 1), :],
+                        row,
+                        mask=(low, high)[i // 2],
                     )
             return carry
 
-        lax.fori_loop(0, TILES, body, 0)
+        lax.fori_loop(0, BLOCKS, body, 0)
 
     def two(i, carry):
         phase(2 * i, 0, g0_ref, g1_ref, True)
@@ -171,12 +180,13 @@
     lax.fori_loop(0, (STEPS - 1) // 2, two, 0)
     phase(STEPS - 1, 0, g0_ref, g1_ref, False)
     low_tile = low_lanes(128)
+    scale, shift = (jnp.concatenate([ref[...]] * 2, axis=1) for ref in (scale_ref, shift_ref))
 
     def finish(t, carry):
         at = pl.ds(pl.multiple_of(t * TILE, TILE), TILE)
         total = acc_ref[at, :] + product(g0_ref, at, STEPS)
         total = total + pltpu.roll(total, CH, 1)
-        fine = jnp.maximum(scale_ref[...] * total + shift_ref[...], 0.0)
+        fine = jnp.maximum(scale * total + shift, 0.0)
         rows_ref[at, :] = fine
         turned = jnp.where(low_tile, fine[:128], fine[128:]).T
         fine_ref[:, pl.ds(pl.multiple_of(t * TILE, TILE), 128)] = turned[:CH]
@@ -201,43 +211,69 @@
             pltpu.VMEM((ROWS, 128), F32),
             pltpu.VMEM((ROWS, 128), F32),
             pltpu.VMEM((VOX, 128), F32),
-            pltpu.SMEM((2, 2, 1, PAIRS), jnp.int32),
-            pltpu.SMEM((2, 2, 1, PAIRS), jnp.int32),
             pltpu.SemaphoreType.DMA,
             pltpu.SemaphoreType.DMA,
-            pltpu.SemaphoreType.DMA((2,)),
-            pltpu.SemaphoreType.DMA((2,)),
-        ],
+            pltpu.SemaphoreType.DMA((2, 8)),
+        ]
+        + [pltpu.SMEM((2, BLOCKS, 128), jnp.int32)] * 8,
         compiler_params=params(48),
         name="conv",
     )(place, own, mid, far, ins, outs, weights, scale, shift)
 
 
-def pack_kernel(rows_ref, table_ref, out_ref):
+SPLIT = OWNERS // 2
+SLOT_SCRATCH = [pltpu.SemaphoreType.DMA((2,))] + [pltpu.SMEM((SPLIT, CAP), jnp.int32)] * 2
+
+
+def slot_tables(table_ref, sem, refs):
+    copies = [
+        pltpu.make_async_copy(table_ref.at[pl.ds(i * SPLIT, SPLIT), :], ref, sem.at[i])
+        for i, ref in enumerate(refs)
+    ]
+    for copy in copies:
+        copy.start()
+    for copy in copies:
+        copy.wait()
+
+
+def pack_kernel(chunk, rows_ref, table_ref, out_ref, sem, *refs):
+    slot_tables(table_ref, sem, refs)
     low = low_lanes()
 
     def owner(a, carry):
-        for r in range(HALF):
-            first = rows_ref[pl.ds(table_ref[a, r], 1), :]
-            second = rows_ref[pl.ds(table_ref[a, r + HALF], 1), :]
-            out_ref[a, pl.ds(r, 1), :] = jnp.where(low, first, second)
-        return carry
-
-    lax.fori_loop(0, OWNERS, owner, 0)
-
-
-def pack(rows, table):
+        for u in range(PART):
+            r = chunk * PART + u
+            for half, ref in enumerate(refs):
+                first = rows_ref[pl.ds(ref[a, r], 1), :]
+                second = rows_ref[pl.ds(ref[a, r + HALF], 1), :]
+                out_ref[a + half * SPLIT, pl.ds(u, 1), :] = jnp.where(low, first, second)
+        return carry
+
+    lax.fori_loop(0, SPLIT, owner, 0)
+
+
+def pack(rows, table, chunk):
     return pl.pallas_call(
-        pack_kernel,
-        out_shape=jax.ShapeDtypeStruct((OWNERS, HALF, 128), F32),
-        in_specs=[VMEM, SMEM],
+        functools.partial(pack_kernel, chunk),
+        out_shape=jax.ShapeDtypeStruct((OWNERS, PART, 128), F32),
+        in_specs=[VMEM, ANY],
         out_specs=VMEM,
-        compiler_params=params(32),
-        name="pack",
+        scratch_shapes=SLOT_SCRATCH,
+        compiler_params=params(16),
+        cost_estimate=pl.CostEstimate(flops=0, bytes_accessed=10 * MIB, transcendentals=0),
+        name=f"pack{chunk}",
     )(rows, table)
 
 
-def down_kernel(x_ref, cols_ref, w_ref, scale_ref, shift_ref, out_ref, p0_ref, p1_ref, *z_refs):
+def down_kernel(chunk, first, last, *args):
+    ins, rest = args[: 3 if first else 4], args[3 if first else 4 :]
+    x_ref, cols_ref, w_ref = ins[:3]
+    if last:
+        scale_ref, shift_ref, *rest = rest
+    out_ref, sem, c0_ref, c1_ref, p0_ref, p1_ref, *z_refs = rest
+    refs = (c0_ref, c1_ref)
+    slot_tables(cols_ref, sem, refs)
+
     def clear(t, carry):
         at = pl.ds(pl.multiple_of(t * 128, 128), 128)
         for z_ref in z_refs:
@@ -245,50 +281,75 @@
         return carry
 
     lax.fori_loop(0, COARSE // 128, clear, 0)
+    for g in range(GROUPS):
+
+        def multiply(i, carry):
+            x = x_ref[pl.ds(i * 8, 8), pl.ds(g * GROUP, GROUP), :].reshape(8 * GROUP, 128)
+            hi, lo = split(x)
+            part = jnp.dot(hi, w_ref[0, chunk * GROUPS + g], preferred_element_type=F32)
+            part += jnp.dot(lo, w_ref[0, chunk * GROUPS + g], preferred_element_type=F32)
+            part += jnp.dot(hi, w_ref[1, chunk * GROUPS + g], preferred_element_type=F32)
+            at = pl.ds(pl.multiple_of((g * OWNERS + i * 8) * GROUP, 8 * GROUP), 8 * GROUP)
+            p0_ref[at, :] = part[:, :128]
+            p1_ref[at, :] = part[:, 128:]
+            return carry
+
+        lax.fori_loop(0, OWNERS // 8, multiply, 0)
 
     def source(s, carry):
-        for c in range(4):
-            hi, lo = split(x_ref[s, pl.ds(c * GROUP, GROUP), :])
-            part = jnp.dot(hi, w_ref[0, c], preferred_element_type=F32)
-            part += jnp.dot(lo, w_ref[0, c], preferred_element_type=F32)
-            part += jnp.dot(hi, w_ref[1, c], preferred_element_type=F32)
-            p0_ref[pl.ds(c * GROUP, GROUP), :] = part[:, :128]
-            p1_ref[pl.ds(c * GROUP, GROUP), :] = part[:, 128:]
-        for r in range(0, HALF, ACCS // 2):
+        for u in range(0, PART, ACCS // 4):
             todo = []
-            for u in range(ACCS // 2):
-                for j, p_ref in enumerate((p0_ref, p1_ref)):
-                    at = pl.ds(cols_ref[s, r + u + j * HALF], 1)
-                    z_ref = z_refs[2 * u + j]
-                    todo.append((z_ref, at, z_ref[at, :] + p_ref[pl.ds(r + u, 1), :]))
+            for k in range(ACCS // 4):
+                group, place = divmod(u + k, GROUP)
+                for i in range(4):
+                    row = (group * OWNERS + s + i % 2 * SPLIT) * GROUP + place
+                    at = pl.ds(refs[i % 2][s, chunk * PART + u + k + i // 2 * HALF], 1)
+                    z_ref = z_refs[4 * k + i]
+                    todo.append((z_ref, at, z_ref[at, :] + (p0_ref, p1_ref)[i // 2][pl.ds(row, 1), :]))
             for z_ref, at, value in todo:
                 z_ref[at, :] = value
         return carry
 
-    lax.fori_loop(0, OWNERS, source, 0)
+    lax.fori_loop(0, SPLIT, source, 0)
 
     def finish(t, carry):
         at = pl.ds(pl.multiple_of(t * 128, 128), 128)
         total = z_refs[0][at, :]
         for z_ref in z_refs[1:]:
             total = total + z_ref[at, :]
-        out_ref[:, at] = jnp.maximum(scale_ref[...] * total + shift_ref[...], 0.0).T
+        if not first:
+            total = total + ins[3][at, :]
+        if last:
+            out_ref[:, at] = jnp.maximum(scale_ref[...] * total + shift_ref[...], 0.0).T
+        else:
+            out_ref[at, :] = total
         return carry
 
     lax.fori_loop(0, COARSE // 128, finish, 0)
 
 
-def down(arrived, cols, weights, scale, shift):
+def down(chunk, arrived, cols, weights, before, scale, shift):
+    last = chunk == CHUNKS - 1
+    operands = [arrived, cols, weights]
+    specs = [VMEM, ANY, VMEM]
+    if before is not None:
+        operands.append(before)
+        specs.append(VMEM)
+    if last:
+        operands += [scale, shift]
+        specs += [VMEM, VMEM]
     return pl.pallas_call(
-        down_kernel,
-        out_shape=jax.ShapeDtypeStruct((CHO, COARSE), F32),
-        in_specs=[VMEM, SMEM, VMEM, VMEM, VMEM],
+        functools.partial(down_kernel, chunk, before is None, last),
+        out_shape=jax.ShapeDtypeStruct((CHO, COARSE) if last else (COARSE, CHO), F32),
+        in_specs=specs,
         out_specs=VMEM,
-        scratch_shapes=[pltpu.VMEM((HALF, 128), F32)] * 2
+        scratch_shapes=SLOT_SCRATCH
+        + [pltpu.VMEM((OWNERS * PART, 128), F32)] * 2
         + [pltpu.VMEM((COARSE + 8, 128), F32)] * ACCS,
-        compiler_params=params(48),
-        name="down",
-    )(arrived, cols, weights, scale, shift)
+        compiler_params=params(40),
+        cost_estimate=pl.CostEstimate(flops=0, bytes_accessed=20 * MIB, transcendentals=0),
+        name=f"down{chunk}",
+    )(*operands)
 
 
 def neighbours(axis, block):
@@ -298,35 +359,41 @@
     return lax.ppermute(block, axis, forward), lax.ppermute(block, axis, backward)
 
 
-def two_parts(w):
-    hi = lax.reduce_precision(w, 8, 7)
-    return hi.astype(BF16), (w - hi).astype(BF16)
-
-
-def conv_weights(w):
-    hi, lo = two_parts(jnp.swapaxes(w, 1, 2))
-    top = jnp.concatenate([hi, lo], axis=2)
-    bottom = jnp.concatenate([hi, jnp.zeros_like(hi)], axis=2)
-
-    def arrange(x):
-        pairs = jnp.concatenate([x[:13], x[14:]], axis=0).reshape(STEPS, 128, 128)
-        centre = jnp.concatenate([x[13], jnp.zeros_like(x[13])], axis=0)
-        return jnp.concatenate([centre[None], pairs], axis=0)
-
-    return jnp.concatenate([arrange(top), arrange(bottom)], axis=1)
-
-
-def down_weights(w):
-    turned = jnp.swapaxes(w, 1, 2)
-    zero = jnp.zeros_like(turned[:4])
-    both = jnp.concatenate(
-        [
-            jnp.concatenate([turned[:4], zero], axis=2),
-            jnp.concatenate([zero, turned[4:]], axis=2),
-        ],
-        axis=1,
-    )
-    return jnp.stack(two_parts(both))
+def weights_kernel(conv_ref, down_ref, conv_out_ref, down_out_ref):
+    empty = jnp.zeros((CH, 128), F32)
+    for s in range(STEPS + 1):
+        if s == 0:
+            first, second = conv_ref[13], jnp.zeros((CH, CH), F32)
+        else:
+            first, second = (conv_ref[k + (k >= 13)] for k in (2 * s - 2, 2 * s - 1))
+        both = jnp.concatenate([first, second], axis=1)
+        hi = both.astype(BF16).astype(F32)
+        top = jnp.concatenate([hi, both - hi], axis=0)
+        bottom = jnp.concatenate([hi, empty], axis=0)
+        conv_out_ref[s, :128, :] = top.T.astype(BF16)
+        conv_out_ref[s, 128:, :] = bottom.T.astype(BF16)
+    left = lax.broadcasted_iota(jnp.int32, (128, CHO), 0) < CH
+    for c in range(4):
+        both = jnp.concatenate([down_ref[c], down_ref[c + 4]], axis=1).T
+        for i, part in enumerate(split(both)):
+            part = part.astype(F32)
+            down_out_ref[i, c, :, :CHO] = jnp.where(left, part, 0.0).astype(BF16)
+            down_out_ref[i, c, :, CHO:] = jnp.where(left, 0.0, part).astype(BF16)
+
+
+def arrange_weights(conv_weight, down_weight):
+    return pl.pallas_call(
+        weights_kernel,
+        out_shape=(
+            jax.ShapeDtypeStruct((STEPS + 1, 256, 128), BF16),
+            jax.ShapeDtypeStruct((2, 4, 128, 2 * CHO), BF16),
+        ),
+        in_specs=[VMEM, VMEM],
+        out_specs=(VMEM, VMEM),
+        compiler_params=params(16),
+        cost_estimate=pl.CostEstimate(flops=0, bytes_accessed=10 * MIB, transcendentals=0),
+        name="weights",
+    )(conv_weight, down_weight)
 
 
 def body(
@@ -343,6 +410,7 @@
     scale_two,
     shift_two,
 ):
+    conv_weight, down_weight = arrange_weights(conv_weight, down_weight)
     own, buf = prep(features[0, 0, 0], boundary_rows[0, 0])
     left, right = neighbours("gx", buf)
     line = jnp.stack([left, buf, right])
@@ -355,21 +423,19 @@
         own,
         mid,
         far,
-        in_maps[0, 0, 0].reshape(26, 1, PAIRS),
-        out_maps[0, 0, 0].reshape(26, 1, PAIRS),
-        conv_weights(conv_weight),
-        jnp.tile(scale_one, 2)[None],
-        jnp.tile(shift_one, 2)[None],
+        in_maps[0, 0, 0].reshape(STEPS, 2, 2, BLOCKS, 128),
+        out_maps[0, 0, 0].reshape(STEPS, 2, 2, BLOCKS, 128),
+        conv_weight,
+        scale_one[None],
+        shift_one[None],
     )
-    packed = pack(rows, send_rows[0, 0, 0])
-    arrived = lax.all_to_all(packed, "gx", split_axis=0, concat_axis=0, tiled=True)
-    coarse = down(
-        arrived,
-        recv_coarse[0, 0, 0],
-        down_weights(down_weight),
-        scale_two[None],
-        shift_two[None],
-    )
+    coarse = None
+    for chunk in range(CHUNKS):
+        packed = pack(rows, send_rows[0, 0, 0], chunk)
+        arrived = lax.all_to_all(packed, "gx", split_axis=0, concat_axis=0, tiled=True)
+        coarse = down(
+            chunk, arrived, recv_coarse[0, 0, 0], down_weight, coarse, scale_two[None], shift_two[None]
+        )
     return (fine[None, None, None], coarse[None, None, None])
 
 

time: 348 us -> 270 us (0.78)
  Pallas kernels: 225 us -> 155 us
  waiting for transfers between devices: 87.1 us -> 68 us
  starting transfers between devices: 21.8 us -> 30.7 us
    pallas_call x1, Pallas kernels: 178 us -> 113 us  [conv(): pl.pallas_call(conv_kernel, out_shape=(jax.ShapeDtypeStruct((CH, VOX), F3...]
    all_to_all x1 -> x2, waiting for transfers between devices: 72 us -> 57.5 us  [body(): lax.all_to_all(packed, 'gx', split_axis=0, concat_axis=0, tiled=True)]
    all_to_all x1 -> x2, starting transfers between devices: 10.8 us -> 18.9 us  [body(): lax.all_to_all(packed, 'gx', split_axis=0, concat_axis=0, tiled=True)]
    ppermute x2, waiting for transfers between devices: 7.31 us -> 3.27 us  [neighbours(): lax.ppermute(block, axis, forward)]
    pallas_call x2 -> x5, Pallas kernels: 43.4 us -> 39.4 us  [the longest x2 26 us: down(): pl.pallas_call(functools.partial(down_kernel, chunk, before is None, last...]
    unnamed x31 -> x37, local copies, waits for them, and re-layouts: 8.5 us -> 11.2 us
  transfers between devices with their start and end apart: 6 -> 7, of which waited for: 6 -> 6; matrix products, arithmetic and copies ran while one was open for 1% -> 1% of each run, Pallas kernels for 0% -> 7%
where the time goes in v2:
time: 270 us; the launch traced here: 269 us
  Pallas kernels  155 us (57%)
  waiting for transfers between devices  68 us (25%)
  starting transfers between devices  30.7 us (11%)
  local copies, waits for them, and re-layouts  11.4 us (4%)
  other arithmetic  2.7 us (1%)
    pallas_call x1, Pallas kernels, conv(): pl.pallas_call(conv_kernel, out_shape=(jax.ShapeDtypeStruct((CH, VOX), F3...  113 us
    all_to_all x2, waiting for transfers between devices, body(): lax.all_to_all(packed, 'gx', split_axis=0, concat_axis=0, tiled=True)  57.5 us
    pallas_call x2, Pallas kernels, down(): pl.pallas_call(functools.partial(down_kernel, chunk, before is None, last...  26 us
    all_to_all x2, starting transfers between devices, body(): lax.all_to_all(packed, 'gx', split_axis=0, concat_axis=0, tiled=True)  18.9 us
    pallas_call x2, Pallas kernels, pack(): pl.pallas_call(functools.partial(pack_kernel, chunk), out_shape=jax.Shape...  12.6 us
    unnamed x37, local copies, waits for them, and re-layouts  11.2 us
    ppermute x2, waiting for transfers between devices, neighbours(): lax.ppermute(block, axis, backward)  7.22 us
    ppermute x2, starting transfers between devices, neighbours(): lax.ppermute(block, axis, forward)  6.47 us
  transfers between devices with their start and end apart: 7, of which 6 were waited for; matrix products, arithmetic and copies ran while one was open for 1% of the time, Pallas kernels for 7%

profile of v2, /device:TPU:8, one launch (start us, length us, event | category | flops | bytes accessed | tf_op | source)
XLA Modules:
  0.0 269.1 jit_solution(819671062440269780)
XLA Ops:
  0.6 1.4 copy-done.8
  2.0 0.7 copy-done.12
  2.7 3.4 %prep.1 = (f32[6144,128]{1,0:T(8,128)S(1)}, f32[256,128]{1,0:T(8,128)S(1)}) custom-call(f32[64,6144]{1,0:T(8,128)S(1)} %bitcast.21, s32[1,512]{1,0:T(1,128)S(1)} %bitcast.27), custom_call_target="tpu_custom_call" | custom-call | tf_op jit(solution)/shard_map/prep/pallas_call | solution.py:77
  6.1 1.3 collective-permute-start.1
  7.4 4.6 %collective-permute-start = (f32[256,128]{1,0:T(8,128)S(1)}, f32[256,128]{1,0:T(8,128)S(1)}, u32[]{:S(2)}, u32[]{:S(2)}) collective-permute-start(f32[256,128]{1,0:T(8,128)S(1)} %get-tuple-element.9), channel_id=1, source_target_pairs={{0,8},{8,16},{16,24},{24,32},{32,40},{40,48},{48,56},{56,64},{64,7... | collective-permute-start | bytes 393224 | tf_op jit(solution)/shard_map/ppermute | solution.py:359
  12.0 1.5 collective-permute-done.1
  13.5 1.2 collective-permute-done
  14.7 4.0 %collective-permute-start.3 = (f32[3,256,128]{2,1,0:T(8,128)S(1)}, f32[3,256,128]{2,1,0:T(8,128)S(1)}, u32[]{:S(2)}, u32[]{:S(2)}) collective-permute-start(f32[3,256,128]{2,1,0:T(8,128)S(1)} %get-tuple-element.15), channel_id=1, source_target_pairs={{2,0},{4,2},{6,4},{3,1},{5,3},{7,5},{10,8},{12,10},{14,12},{11,9},... | collective-permute-start | bytes 1179656 | tf_op jit(solution)/shard_map/ppermute | solution.py:359
  18.7 1.9 collective-permute-start.2
  20.6 5.8 %collective-permute-done.3 = f32[3,256,128]{2,1,0:T(8,128)S(1)} collective-permute-done((f32[3,256,128]{2,1,0:T(8,128)S(1)}, f32[3,256,128]{2,1,0:T(8,128)S(1)}, u32[]{:S(2)}, u32[]{:S(2)}) %collective-permute-start.3) | collective-permute-done | bytes 393248 | tf_op jit(solution)/shard_map/ppermute | solution.py:359
  26.3 2.1 collective-permute-done.2
  28.7 0.8 copy-done.17
  29.5 0.8 reduce
  30.3 0.1 reshape_squeeze.6.ins_ref
  30.4 1.8 reduce.1
  32.3 1.2 copy.17.down_ref
  33.5 0.8 weights.1
  34.3 0.8 copy-done.5
  35.2 112.5 %conv.1 = (f32[64,6144]{1,0:T(8,128)}, f32[6152,128]{1,0:T(8,128)}) custom-call(s32[1]{0:T(128)} %bitcast.place_ref, f32[6144,128]{1,0:T(8,128)} %copy-done.4, f32[9,256,128]{2,1,0:T(8,128)S(1)} %bitcast.20, f32[9,256,128]{2,1,0:T(8,128)} %collective-permute-done.4.far_ref, s32[13,2,2,12,128]{4,3,2,1,0:T(8,128)S(1)} %reshape_squeeze.6.ins_ref, ...), custom_call_target="tpu_custom_call" | custom-call | tf_op jit(solution)/shard_map/conv/pallas_call | solution.py:201
  147.8 1.9 copy-done
  149.6 6.3 %pack0.1 = f32[32,96,128]{2,1,0:T(8,128)S(1)} custom-call(f32[6152,128]{1,0:T(8,128)S(1)} %copy-done, s32[32,384]{1,0:T(8,128)S(1)} %bitcast.22), custom_call_target="tpu_custom_call" | custom-call | bytes 10485760 | tf_op jit(solution)/shard_map/pack0/pallas_call | solution.py:256
  155.9 1.2 copy-done.3
  157.1 13.3 %all-to-all-start.1 = ((f32[32,96,128]{2,1,0:T(8,128)}), f32[32,96,128]{2,1,0:T(8,128)}, u32[]{:S(2)}, u32[]{:S(2)}) async-start(f32[32,96,128]{2,1,0:T(8,128)} %copy-done.3), calls=%async_computation.1 | async-start | bytes 3145728 | tf_op jit(solution)/shard_map/all_to_all | solution.py:435
  170.5 6.3 %pack1.1 = f32[32,96,128]{2,1,0:T(8,128)S(1)} custom-call(f32[6152,128]{1,0:T(8,128)S(1)} %copy-done.1, s32[32,384]{1,0:T(8,128)S(1)} %bitcast.23), custom_call_target="tpu_custom_call" | custom-call | bytes 10485760 | tf_op jit(solution)/shard_map/pack1/pallas_call | solution.py:256
  176.8 1.1 copy-done.2
  177.9 31.8 %all-to-all-done.1.args_0_ = f32[32,96,128]{2,1,0:T(8,128)} async-done(((f32[32,96,128]{2,1,0:T(8,128)}), f32[32,96,128]{2,1,0:T(8,128)}, u32[]{:S(2)}, u32[]{:S(2)}) %all-to-all-start.1) | async-done | bytes 1572896 | tf_op jit(solution)/shard_map/all_to_all | solution.py:435
  209.7 5.6 %all-to-all-start = ((f32[32,96,128]{2,1,0:T(8,128)}), f32[32,96,128]{2,1,0:T(8,128)S(1)}, u32[]{:S(2)}, u32[]{:S(2)}) async-start(f32[32,96,128]{2,1,0:T(8,128)} %copy-done.2), calls=%async_computation | async-start | bytes 3145728 | tf_op jit(solution)/shard_map/all_to_all | solution.py:435
  215.3 1.0 copy-done.6
  216.3 12.2 %down0.1.args_3_ = f32[3072,128]{1,0:T(8,128)S(1)} custom-call(f32[32,96,128]{2,1,0:T(8,128)} %all-to-all-done.1.args_0_, s32[32,384]{1,0:T(8,128)S(1)} %bitcast.24, bf16[2,4,128,256]{3,2,1,0:T(8,128)(2,1)S(1)} %copy-done.6), custom_call_target="tpu_custom_call" | custom-call | bytes 20971520 | tf_op jit(solution)/shard_map/down0/pallas_call | solution.py:341
  228.5 25.7 %all-to-all-done.args_0_ = f32[32,96,128]{2,1,0:T(8,128)S(1)} async-done(((f32[32,96,128]{2,1,0:T(8,128)}), f32[32,96,128]{2,1,0:T(8,128)S(1)}, u32[]{:S(2)}, u32[]{:S(2)}) %all-to-all-start) | async-done | bytes 1572896 | tf_op jit(solution)/shard_map/all_to_all | solution.py:435
  254.2 1.0 copy-done.7
  255.3 13.9 %down1.1 = f32[128,3072]{1,0:T(8,128)} custom-call(f32[32,96,128]{2,1,0:T(8,128)S(1)} %all-to-all-done.args_0_, s32[32,384]{1,0:T(8,128)S(1)} %bitcast.25, bf16[2,4,128,256]{3,2,1,0:T(8,128)(2,1)S(1)} %copy-done.7, f32[3072,128]{1,0:T(8,128)S(1)} %down0.1.args_3_, f32[1,128]{1,0:T(1,128)S(1)} %bitcast.30, f32[1,128]{1,0:T(1,128)S(1)} %bitcast.31), custom_call_target="tpu_custom_call" | custom-call | bytes 20971520 | tf_op jit(solution)/shard_map/down1/pallas_call | solution.py:341
  (33 shorter events, 0.5 us)
Async XLA Ops:
  0.6 1.4 copy-start.8
  2.0 0.7 copy-start.12
  6.1 22.4 %copy-start.4 = (f32[6144,128]{1,0:T(8,128)}, f32[6144,128]{1,0:T(8,128)S(1)}, u32[]{:S(2)}) copy-start(f32[6144,128]{1,0:T(8,128)S(1)} %get-tuple-element.8.own_ref) | copy-start | bytes 9437188
  6.1 7.3 %collective-permute-start.1 = (f32[256,128]{1,0:T(8,128)S(1)}, f32[256,128]{1,0:T(8,128)S(1)}, u32[]{:S(2)}, u32[]{:S(2)}) collective-permute-start(f32[256,128]{1,0:T(8,128)S(1)} %get-tuple-element.9), channel_id=1, source_target_pairs={{8,0},{16,8},{24,16},{32,24},{40,32},{48,40},{56,48},{64,56},{72,6... | collective-permute-start | bytes 393224 | tf_op jit(solution)/shard_map/ppermute | solution.py:359
  7.4 7.2 %collective-permute-start = (f32[256,128]{1,0:T(8,128)S(1)}, f32[256,128]{1,0:T(8,128)S(1)}, u32[]{:S(2)}, u32[]{:S(2)}) collective-permute-start(f32[256,128]{1,0:T(8,128)S(1)} %get-tuple-element.9), channel_id=1, source_target_pairs={{0,8},{8,16},{16,24},{24,32},{32,40},{40,48},{48,56},{56,64},{64,7... | collective-permute-start | bytes 393224 | tf_op jit(solution)/shard_map/ppermute | solution.py:359
  14.7 11.7 %collective-permute-start.3 = (f32[3,256,128]{2,1,0:T(8,128)S(1)}, f32[3,256,128]{2,1,0:T(8,128)S(1)}, u32[]{:S(2)}, u32[]{:S(2)}) collective-permute-start(f32[3,256,128]{2,1,0:T(8,128)S(1)} %get-tuple-element.15), channel_id=1, source_target_pairs={{2,0},{4,2},{6,4},{3,1},{5,3},{7,5},{10,8},{12,10},{14,12},{11,9},... | collective-permute-start | bytes 1179656 | tf_op jit(solution)/shard_map/ppermute | solution.py:359
  18.7 9.8 %collective-permute-start.2 = (f32[3,256,128]{2,1,0:T(8,128)S(1)}, f32[3,256,128]{2,1,0:T(8,128)S(1)}, u32[]{:S(2)}, u32[]{:S(2)}) collective-permute-start(f32[3,256,128]{2,1,0:T(8,128)S(1)} %get-tuple-element.15), channel_id=1, source_target_pairs={{0,2},{2,4},{4,6},{1,3},{3,5},{5,7},{8,10},{10,12},{12,14},{9,11},... | collective-permute-start | bytes 1179656 | tf_op jit(solution)/shard_map/ppermute | solution.py:359
  28.5 1.0 copy-start.17
  28.6 6.5 %collective-permute-start.4 = (f32[9,256,128]{2,1,0:T(8,128)S(1)}, f32[9,256,128]{2,1,0:T(8,128)}, u32[]{:S(2)}, u32[]{:S(2)}) collective-permute-start(f32[9,256,128]{2,1,0:T(8,128)S(1)} %bitcast.19), channel_id=1, source_target_pairs={{0,1},{1,0},{2,3},{3,2},{4,5},{5,4},{6,7},{7,6},{8,9},{9,8},{10,11... | collective-permute-start | bytes 3538952 | tf_op jit(solution)/shard_map/ppermute | solution.py:419
  30.3 3.2 %copy-start.9 = (f32[27,64,64]{2,1,0:T(8,128)S(1)}, f32[27,64,64]{2,1,0:T(8,128)}, u32[]{:S(2)}) copy-start(f32[27,64,64]{2,1,0:T(8,128)} %conv_ref.1) | copy-start | bytes 1327108
  32.2 3.0 %copy-start.13 = (f32[64]{0:T(128)S(1)}, f32[64]{0:T(128)}, u32[]{:S(2)}) copy-start(f32[64]{0:T(128)} %param.19) | copy-start | bytes 772
  32.2 3.0 %copy-start.14 = (f32[64]{0:T(128)S(1)}, f32[64]{0:T(128)}, u32[]{:S(2)}) copy-start(f32[64]{0:T(128)} %param.20) | copy-start | bytes 772
  34.3 0.8 copy-start.5
  35.2 112.6 %copy-start.10 = (s32[1,1,1,32,384]{4,3,2,1,0:T(8,128)S(1)}, s32[1,1,1,32,384]{4,3,2,1,0:T(8,128)}, u32[]{:S(2)}) copy-start(s32[1,1,1,32,384]{4,3,2,1,0:T(8,128)} %param.16) | copy-start | bytes 147460
  147.7 1.9 copy-start
  149.6 20.8 %copy-start.1 = (f32[6152,128]{1,0:T(8,128)S(1)}, f32[6152,128]{1,0:T(8,128)}, u32[]{:S(2)}) copy-start(f32[6152,128]{1,0:T(8,128)} %get-tuple-element.12.rows_ref) | copy-start | bytes 9449476
  155.9 1.2 copy-start.3
  157.1 52.6 %all-to-all-start.1 = ((f32[32,96,128]{2,1,0:T(8,128)}), f32[32,96,128]{2,1,0:T(8,128)}, u32[]{:S(2)}, u32[]{:S(2)}) async-start(f32[32,96,128]{2,1,0:T(8,128)} %copy-done.3), calls=%async_computation.1 | async-start | bytes 3145728 | tf_op jit(solution)/shard_map/all_to_all | solution.py:435
  176.7 1.1 copy-start.2
  177.9 37.4 %copy-start.11 = (s32[1,1,1,32,384]{4,3,2,1,0:T(8,128)S(1)}, s32[1,1,1,32,384]{4,3,2,1,0:T(8,128)}, u32[]{:S(2)}) copy-start(s32[1,1,1,32,384]{4,3,2,1,0:T(8,128)} %param.17) | copy-start | bytes 147460
  209.7 44.5 %all-to-all-start = ((f32[32,96,128]{2,1,0:T(8,128)}), f32[32,96,128]{2,1,0:T(8,128)S(1)}, u32[]{:S(2)}, u32[]{:S(2)}) async-start(f32[32,96,128]{2,1,0:T(8,128)} %copy-done.2), calls=%async_computation | async-start | bytes 3145728 | tf_op jit(solution)/shard_map/all_to_all | solution.py:435
  215.3 1.0 copy-start.6
  216.3 37.9 %copy-start.15 = (f32[128]{0:T(128)S(1)}, f32[128]{0:T(128)}, u32[]{:S(2)}) copy-start(f32[128]{0:T(128)} %param.22) | copy-start | bytes 1540
  216.3 37.9 %copy-start.16 = (f32[128]{0:T(128)S(1)}, f32[128]{0:T(128)}, u32[]{:S(2)}) copy-start(f32[128]{0:T(128)} %param.23) | copy-start | bytes 1540
  254.2 1.0 copy-start.7

commit v3 on v2

v3 whole, which is shorter than its diff:
```python
import functools

import jax
import jax.numpy as jnp
from jax import lax
from jax.experimental import pallas as pl
from jax.experimental.pallas import tpu as pltpu
from jax.sharding import PartitionSpec as P

CH = 64
CHO = 128
VOX = 6144
PAIRS = 3072
BND = 512
COARSE = 3072
OWNERS = 32
CAP = 384
ZERO_ROW = VOX + 27 * BND
TABLE = ZERO_ROW + 8
ROWS = VOX + 8
TILE = 256
TILES = VOX // TILE
BLOCK = 1024
BLOCKS = VOX // BLOCK
CUTS = PAIRS // (128 * BLOCKS)
STEPS = 13
GROUP = 48
HALF = CAP // 2
ACCS = 8
CHUNKS = ((0, 3), (3, 1))
F32 = jnp.float32
BF16 = jnp.bfloat16
MIB = 1 << 20

VMEM = pl.BlockSpec(memory_space=pltpu.VMEM)
SMEM = pl.BlockSpec(memory_space=pltpu.SMEM)
ANY = pl.BlockSpec(memory_space=pl.ANY)


def params(mib):
    return pltpu.CompilerParams(vmem_limit_bytes=mib * MIB)


def low_lanes(rows=1):
    return lax.broadcasted_iota(jnp.int32, (rows, 128), 1) < CH


def split(x):
    hi = x.astype(BF16)
    lo = (x - hi.astype(F32)).astype(BF16)
    return hi, lo


PIECE = VOX // 4


def prep_kernel(own_ref, rows_ref, table_out_ref, buf_ref, x_ref, table_ref, in_sem, out_sem):
    arriving, leaving = [], []
    for i in range(4):
        at = pl.ds(i * PIECE, PIECE)
        arriving.append(pltpu.make_async_copy(own_ref.at[:, at], x_ref.at[:, at], in_sem.at[i]))
        leaving.append(
            pltpu.make_async_copy(table_ref.at[at, :], table_out_ref.at[at, :], out_sem.at[i])
        )
    for copy in arriving:
        copy.start()
    for i in range(4):
        arriving[i].wait()

        def turn(t, carry):
            at = pl.ds(pl.multiple_of(i * PIECE + t * TILE, TILE), TILE)
            x = x_ref[:, at]
            table_ref[at, :] = jnp.concatenate([x, x], axis=0).T
            return carry

        lax.fori_loop(0, PIECE // TILE, turn, 0)
        leaving[i].start()
    low = low_lanes()

    def pick(i, carry):
        for u in range(32):
            r = i * 32 + u
            first = table_ref[pl.ds(rows_ref[0, r], 1), :]
            second = table_ref[pl.ds(rows_ref[0, r + BND // 2], 1), :]
            buf_ref[pl.ds(r, 1), :] = jnp.where(low, first, second)
        return carry

    lax.fori_loop(0, BND // 64, pick, 0)
    for copy in leaving:
        copy.wait()


def prep(own, rows):
    return pl.pallas_call(
        prep_kernel,
        out_shape=(
            jax.ShapeDtypeStruct((VOX, 128), F32),
            jax.ShapeDtypeStruct((BND // 2, 128), F32),
        ),
        in_specs=[ANY, SMEM],
        out_specs=(ANY, VMEM),
        scratch_shapes=[
            pltpu.VMEM((CH, VOX), F32),
            pltpu.VMEM((VOX, 128), F32),
            pltpu.SemaphoreType.DMA((4,)),
            pltpu.SemaphoreType.DMA((4,)),
        ],
        compiler_params=params(60),
        name="prep",
    )(own, rows)


def spread(s_ref, start, buf):
    other = pltpu.roll(buf, CH, 1)
    low = low_lanes(BND // 2)
    s_ref[pl.ds(start, BND // 2), :] = jnp.where(low, buf, other)
    s_ref[pl.ds(start + BND // 2, BND // 2), :] = jnp.where(low, other, buf)


TABLES = 4
SPLIT = OWNERS // TABLES
SLOT_SCRATCH = [pltpu.SemaphoreType.DMA((TABLES,))] + [
    pltpu.SMEM((SPLIT, CAP // 128, 128), jnp.int32)
] * TABLES


def slot_tables(table_ref, sem, refs):
    return [
        pltpu.make_async_copy(table_ref.at[i], ref, sem.at[i]) for i, ref in enumerate(refs)
    ]


def in_quarters(table):
    return table.reshape(TABLES, SPLIT, CAP // 128, 128)


def pack_rows(chunk, rows_ref, refs, out_ref):
    start, groups = chunk
    low = low_lanes()

    def owner(a, carry):
        for u in range(groups * GROUP):
            r = start * GROUP + u
            for part, ref in enumerate(refs):
                first, second = (
                    rows_ref[pl.ds(ref[a, t // 128, t % 128], 1), :] for t in (r, r + HALF)
                )
                out_ref[a + part * SPLIT, pl.ds(u, 1), :] = jnp.where(low, first, second)
        return carry

    lax.fori_loop(0, SPLIT, owner, 0)


def conv_kernel(
    place_ref, own_ref, mid_in_ref, far_in_ref, ins_ref, outs_ref, w_in_ref, norm_ref,
    table_ref, fine_out_ref, rows_out_ref, packed_out_ref,
    s_ref, g0_ref, g1_ref, acc_ref, fine_ref, packed_ref, mid_ref, far_ref, w_ref, in_sem, out_sem, list_sem, *refs,
):
    list_refs, slot_sem, slot_refs = refs[: 4 * CUTS], refs[4 * CUTS], refs[4 * CUTS + 1 :]
    slot_copies = slot_tables(table_ref, slot_sem, slot_refs)
    for copy in slot_copies:
        copy.start()
    mid_copy, far_copy, own_copy, w_copy = (
        pltpu.make_async_copy(source, target, in_sem.at[i])
        for i, (source, target) in enumerate(
            (
                (mid_in_ref, mid_ref),
                (far_in_ref, far_ref),
                (own_ref, s_ref.at[pl.ds(0, VOX), :]),
                (w_in_ref, w_ref),
            )
        )
    )
    for copy in (mid_copy, far_copy, own_copy, w_copy):
        copy.start()

    def lists(s, slot):
        return [
            pltpu.make_async_copy(
                (ins_ref, outs_ref)[i // (2 * CUTS)].at[s, i // CUTS % 2, i % CUTS],
                ref.at[slot],
                list_sem.at[slot, i],
            )
            for i, ref in enumerate(list_refs)
        ]

    for copy in lists(0, 0):
        copy.start()
    def clear(t, carry):
        at = pl.ds(pl.multiple_of(t * TILE, TILE), TILE)
        g0_ref[at, :] = jnp.zeros((TILE, 128), F32)
        acc_ref[at, :] = jnp.zeros((TILE, 128), F32)
        return carry

    lax.fori_loop(0, TILES, clear, 0)
    mid_copy.wait()
    far_copy.wait()
    here = place_ref[0]
    other = 2 - 2 * here
    same = 2 * here
    empty = jnp.zeros((BND, 128), F32)

    def fill(e, carry):
        base = VOX + e * 3 * BND
        spread(s_ref, pl.multiple_of(base + BND, BND), mid_ref[e])
        spread(s_ref, pl.multiple_of(base + other * BND, BND), far_ref[e])
        s_ref[pl.ds(pl.multiple_of(base + same * BND, BND), BND), :] = empty
        return carry

    lax.fori_loop(0, 9, fill, 0)
    s_ref[pl.ds(ZERO_ROW, 8), :] = jnp.zeros((8, 128), F32)

    low = low_lanes()
    high = jnp.logical_not(low)
    own_copy.wait()

    def centre(t, carry):
        at = pl.ds(pl.multiple_of(t * TILE, TILE), TILE)
        g1_ref[at, :] = s_ref[at, :]
        return carry

    lax.fori_loop(0, TILES, centre, 0)
    w_copy.wait()

    def product(ref, at, s):
        hi, lo = split(ref[at, :])
        return jnp.dot(
            jnp.concatenate([hi, lo], axis=1), w_ref[s], preferred_element_type=F32
        )

    def phase(s, slot, now_ref, last_ref, more):
        for copy in lists(s, slot):
            copy.wait()
        if more:
            for copy in lists(s + 1, 1 - slot):
                copy.start()

        def body(t, carry):
            at = pl.ds(pl.multiple_of(t * BLOCK, BLOCK), BLOCK)
            acc_ref[at, :] += product(last_ref, at, s)
            last_ref[at, :] = jnp.zeros((BLOCK, 128), F32)
            for u in range(128):
                for i in range(2 * CUTS):
                    row = s_ref[pl.ds(list_refs[i][slot, t, u], 1), :]
                    pltpu.store(
                        now_ref.at[pl.ds(list_refs[i + 2 * CUTS][slot, t, u], 1), :],
                        row,
                        mask=(low, high)[i // CUTS],
                    )
            return carry

        lax.fori_loop(0, BLOCKS, body, 0)

    def two(i, carry):
        phase(2 * i, 0, g0_ref, g1_ref, True)
        phase(2 * i + 1, 1, g1_ref, g0_ref, True)
        return carry

    lax.fori_loop(0, (STEPS - 1) // 2, two, 0)
    phase(STEPS - 1, 0, g0_ref, g1_ref, False)
    low_tile = low_lanes(128)
    scale, shift = norm_ref[0:1, :], norm_ref[1:2, :]

    def finish(t, carry):
        at = pl.ds(pl.multiple_of(t * TILE, TILE), TILE)
        total = acc_ref[at, :] + product(g0_ref, at, STEPS)
        total = total + pltpu.roll(total, CH, 1)
        fine = jnp.maximum(scale * total + shift, 0.0)
        acc_ref[at, :] = fine
        turned = jnp.where(low_tile, fine[:128], fine[128:]).T
        fine_ref[:, pl.ds(pl.multiple_of(t * TILE, TILE), 128)] = turned[:CH]
        fine_ref[:, pl.ds(pl.multiple_of(t * TILE + 128, 128), 128)] = turned[CH:]
        return carry

    lax.fori_loop(0, TILES, finish, 0)
    acc_ref[pl.ds(VOX, 8), :] = jnp.zeros((8, 128), F32)
    outgoing = [
        pltpu.make_async_copy(acc_ref, rows_out_ref, out_sem.at[0]),
        pltpu.make_async_copy(fine_ref, fine_out_ref, out_sem.at[1]),
    ]
    for copy in slot_copies:
        copy.wait()
    for copy in outgoing:
        copy.start()
    pack_rows(CHUNKS[0], acc_ref, slot_refs, packed_ref)
    packed = pltpu.make_async_copy(packed_ref, packed_out_ref, out_sem.at[2])
    packed.start()
    for copy in (*outgoing, packed):
        copy.wait()


def conv(place, own, mid, far, ins, outs, weights, norm, table):
    packed = (OWNERS, CHUNKS[0][1] * GROUP, 128)
    return pl.pallas_call(
        conv_kernel,
        out_shape=(
            jax.ShapeDtypeStruct((CH, VOX), F32),
            jax.ShapeDtypeStruct((ROWS, 128), F32),
            jax.ShapeDtypeStruct(packed, F32),
        ),
        in_specs=[SMEM, ANY, ANY, ANY, ANY, ANY, ANY, VMEM, ANY],
        out_specs=(ANY, ANY, ANY),
        scratch_shapes=[
            pltpu.VMEM((TABLE, 128), F32),
            pltpu.VMEM((ROWS, 128), F32),
            pltpu.VMEM((ROWS, 128), F32),
            pltpu.VMEM((ROWS, 128), F32),
            pltpu.VMEM((CH, VOX), F32),
            pltpu.VMEM(packed, F32),
            pltpu.VMEM((9, BND // 2, 128), F32),
            pltpu.VMEM((9, BND // 2, 128), F32),
            pltpu.VMEM((STEPS + 1, 256, 128), BF16),
            pltpu.SemaphoreType.DMA((4,)),
            pltpu.SemaphoreType.DMA((3,)),
            pltpu.SemaphoreType.DMA((2, 4 * CUTS)),
        ]
        + [pltpu.SMEM((2, BLOCKS, 128), jnp.int32)] * (4 * CUTS)
        + SLOT_SCRATCH,
        compiler_params=params(60),
        name="conv",
    )(place, own, mid, far, ins, outs, weights, norm, table)


def pack_kernel(chunk, rows_ref, table_ref, out_ref, sem, *refs):
    copies = slot_tables(table_ref, sem, refs)
    for copy in copies:
        copy.start()
    for copy in copies:
        copy.wait()
    pack_rows(chunk, rows_ref, refs, out_ref)


def pack(rows, table, chunk):
    return pl.pallas_call(
        functools.partial(pack_kernel, chunk),
        out_shape=jax.ShapeDtypeStruct((OWNERS, chunk[1] * GROUP, 128), F32),
        in_specs=[VMEM, ANY],
        out_specs=VMEM,
        scratch_shapes=SLOT_SCRATCH,
        compiler_params=params(60),
        cost_estimate=pl.CostEstimate(flops=0, bytes_accessed=10 * MIB, transcendentals=0),
        name=f"pack{chunk[0]}",
    )(rows, table)


def down_kernel(chunk, first, last, *args):
    x_ref, cols_ref, w_ref, norm_ref, *rest = args
    if not first:
        before_in_ref, *rest, before_ref, before_sem = rest
        before_copy = pltpu.make_async_copy(before_in_ref, before_ref, before_sem)
        before_copy.start()
    out_ref, sem, *rest = rest
    refs, (p0_ref, p1_ref, *z_refs) = rest[:TABLES], rest[TABLES:]
    copies = slot_tables(cols_ref, sem, refs)
    for copy in copies:
        copy.start()
    start, groups = chunk

    def clear(t, carry):
        at = pl.ds(pl.multiple_of(t * 128, 128), 128)
        for z_ref in z_refs:
            z_ref[at, :] = jnp.zeros((128, 128), F32)
        return carry

    lax.fori_loop(0, COARSE // 128, clear, 0)
    for g in range(groups):

        def multiply(i, carry):
            x = x_ref[pl.ds(i * 8, 8), pl.ds(g * GROUP, GROUP), :].reshape(8 * GROUP, 128)
            hi, lo = split(x)
            part = jnp.dot(hi, w_ref[0, start + g], preferred_element_type=F32)
            part += jnp.dot(lo, w_ref[0, start + g], preferred_element_type=F32)
            part += jnp.dot(hi, w_ref[1, start + g], preferred_element_type=F32)
            at = pl.ds(pl.multiple_of((g * OWNERS + i * 8) * GROUP, 8 * GROUP), 8 * GROUP)
            p0_ref[at, :] = part[:, :128]
            p1_ref[at, :] = part[:, 128:]
            return carry

        lax.fori_loop(0, OWNERS // 8, multiply, 0)

    def source(s, carry):
        for u in range(groups * GROUP):
            group, place = divmod(u, GROUP)
            todo = []
            for i, z_ref in enumerate(z_refs):
                part, half = i % TABLES, i // TABLES
                row = (group * OWNERS + s + part * SPLIT) * GROUP + place
                t = start * GROUP + u + half * HALF
                at = pl.ds(refs[part][s, t // 128, t % 128], 1)
                todo.append((z_ref, at, z_ref[at, :] + (p0_ref, p1_ref)[half][pl.ds(row, 1), :]))
            for z_ref, at, value in todo:
                z_ref[at, :] = value
        return carry

    for copy in copies:
        copy.wait()
    lax.fori_loop(0, SPLIT, source, 0)

    if not first:
        before_copy.wait()

    def finish(t, carry):
        at = pl.ds(pl.multiple_of(t * 128, 128), 128)
        total = z_refs[0][at, :]
        for z_ref in z_refs[1:]:
            total = total + z_ref[at, :]
        if not first:
            total = total + before_ref[at, :]
        if last:
            out_ref[:, at] = jnp.maximum(norm_ref[2:3, :] * total + norm_ref[3:4, :], 0.0).T
        else:
            out_ref[at, :] = total
        return carry

    lax.fori_loop(0, COARSE // 128, finish, 0)


def down(chunk, arrived, cols, weights, norm, before):
    last = chunk == CHUNKS[-1]
    carried = [] if before is None else [before]
    return pl.pallas_call(
        functools.partial(down_kernel, chunk, before is None, last),
        out_shape=jax.ShapeDtypeStruct((CHO, COARSE) if last else (COARSE, CHO), F32),
        in_specs=[VMEM, ANY, VMEM, VMEM] + [ANY] * len(carried),
        out_specs=VMEM,
        scratch_shapes=SLOT_SCRATCH
        + [pltpu.VMEM((OWNERS * chunk[1] * GROUP, 128), F32)] * 2
        + [pltpu.VMEM((COARSE + 8, 128), F32)] * ACCS
        + [pltpu.VMEM((COARSE, CHO), F32), pltpu.SemaphoreType.DMA] * len(carried),
        compiler_params=params(60),
        cost_estimate=pl.CostEstimate(flops=0, bytes_accessed=20 * MIB, transcendentals=0),
        name=f"down{chunk[0]}",
    )(arrived, cols, weights, norm, *carried)


def neighbours(axis, block):
    count = lax.axis_size(axis)
    forward = [(i, i + 1) for i in range(count - 1)]
    backward = [(target, source) for source, target in forward]
    return lax.ppermute(block, axis, forward), lax.ppermute(block, axis, backward)


def weights_kernel(
    conv_ref, down_ref, scale_one_ref, shift_one_ref, scale_two_ref, shift_two_ref,
    conv_out_ref, down_out_ref, norm_ref,
):
    for i, ref in enumerate((scale_one_ref, shift_one_ref)):
        norm_ref[i : i + 1, :] = jnp.concatenate([ref[...]] * 2, axis=1)
    norm_ref[2:3, :] = scale_two_ref[...]
    norm_ref[3:4, :] = shift_two_ref[...]
    norm_ref[4:8, :] = jnp.zeros((4, 128), F32)
    empty = jnp.zeros((CH, 128), F32)
    for s in range(STEPS + 1):
        if s == 0:
            first, second = conv_ref[13], jnp.zeros((CH, CH), F32)
        else:
            first, second = (conv_ref[k + (k >= 13)] for k in (2 * s - 2, 2 * s - 1))
        both = jnp.concatenate([first, second], axis=1)
        hi = both.astype(BF16).astype(F32)
        top = jnp.concatenate([hi, both - hi], axis=0)
        bottom = jnp.concatenate([hi, empty], axis=0)
        conv_out_ref[s, :128, :] = top.T.astype(BF16)
        conv_out_ref[s, 128:, :] = bottom.T.astype(BF16)
    left = lax.broadcasted_iota(jnp.int32, (128, CHO), 0) < CH
    for c in range(4):
        both = jnp.concatenate([down_ref[c], down_ref[c + 4]], axis=1).T
        for i, part in enumerate(split(both)):
            part = part.astype(F32)
            down_out_ref[i, c, :, :CHO] = jnp.where(left, part, 0.0).astype(BF16)
            down_out_ref[i, c, :, CHO:] = jnp.where(left, 0.0, part).astype(BF16)


def arrange_weights(conv_weight, down_weight, *norms):
    return pl.pallas_call(
        weights_kernel,
        out_shape=(
            jax.ShapeDtypeStruct((STEPS + 1, 256, 128), BF16),
            jax.ShapeDtypeStruct((2, 4, 128, 2 * CHO), BF16),
            jax.ShapeDtypeStruct((8, 128), F32),
        ),
        in_specs=[VMEM] * 6,
        out_specs=(VMEM, VMEM, VMEM),
        compiler_params=params(60),
        cost_estimate=pl.CostEstimate(flops=0, bytes_accessed=10 * MIB, transcendentals=0),
        name="weights",
    )(conv_weight, down_weight, *norms)


def body(
    features,
    boundary_rows,
    in_maps,
    out_maps,
    send_rows,
    recv_coarse,
    conv_weight,
    scale_one,
    shift_one,
    down_weight,
    scale_two,
    shift_two,
):
    conv_weight, down_weight, norm = arrange_weights(
        conv_weight, down_weight, scale_one[None], shift_one[None], scale_two[None], shift_two[None]
    )
    own, buf = prep(features[0, 0, 0], boundary_rows[0, 0])
    left, right = neighbours("gx", buf)
    line = jnp.stack([left, buf, right])
    line, conv_weight, down_weight, norm = lax.optimization_barrier(
        (line, conv_weight, down_weight, norm)
    )
    low, high = neighbours("gy", line)
    ins, outs = (x[0, 0, 0].reshape(STEPS, 2, CUTS, BLOCKS, 128) for x in (in_maps, out_maps))
    places, cols = in_quarters(send_rows[0, 0, 0]), in_quarters(recv_coarse[0, 0, 0])
    low, high, ins, outs, places, cols = lax.optimization_barrier(
        (low, high, ins, outs, places, cols)
    )
    mid = jnp.stack([low, line, high], axis=1).reshape(9, BND // 2, 128)
    far = lax.ppermute(mid, "gz", [(0, 1), (1, 0)])
    place = lax.axis_index("gz").astype(jnp.int32).reshape(1)
    fine, rows, packed = conv(
        place,
        own,
        mid,
        far,
        ins,
        outs,
        conv_weight,
        norm,
        places,
    )
    coarse = None
    for chunk in CHUNKS:
        if chunk != CHUNKS[0]:
            packed = pack(rows, places, chunk)
        arrived = lax.all_to_all(packed, "gx", split_axis=0, concat_axis=0, tiled=True)
        coarse = down(chunk, arrived, cols, down_weight, norm, coarse)
    return (fine[None, None, None], coarse[None, None, None])


def solution(mesh):
    return jax.shard_map(
        body,
        mesh=mesh,
        in_specs=(
            P("gx", "gy", "gz", None, None),
            P("gx", "gy", "gz", None),
            P("gx", "gy", "gz", None, None),
            P("gx", "gy", "gz", None, None),
            P("gx", "gy", "gz", None, None),
            P("gx", "gy", "gz", None, None),
            P(),
            P(),
            P(),
            P(),
            P(),
            P(),
        ),
        out_specs=(P("gx", "gy", "gz", None, None), P("gx", "gy", "gz", None, None)),
        check_vma=False,
    )
```

time: 270 us -> 262 us (0.970)
  local copies, waits for them, and re-layouts: 11.4 us -> 6.78 us
  waiting for transfers between devices: 68 us -> 64.9 us
    unnamed x37 -> x21, local copies, waits for them, and re-layouts: 11.2 us -> 3.57 us
    pallas_call x2 -> x1, Pallas kernels: 12.6 us -> 6.13 us  [pack(): pl.pallas_call(functools.partial(pack_kernel, chunk), out_shape=jax.Shape...]
    pallas_call x1, Pallas kernels: 113 us -> 115 us  [conv(): pl.pallas_call(conv_kernel, out_shape=(jax.ShapeDtypeStruct((CH, VOX), F3...]
  transfers between devices with their start and end apart: 7 -> 7, of which waited for: 6 -> 6; matrix products, arithmetic and copies ran while one was open for 1% -> 2% of each run, Pallas kernels for 7% -> 10%
where the time goes in v3:
time: 262 us; the launch traced here: 261 us
  Pallas kernels  157 us (60%)
  waiting for transfers between devices  64.9 us (25%)
  starting transfers between devices  29.8 us (11%)
  local copies, waits for them, and re-layouts  6.78 us (3%)
    pallas_call x1, Pallas kernels, conv(): pl.pallas_call(conv_kernel, out_shape=(jax.ShapeDtypeStruct((CH, VOX), F3...  115 us
    all_to_all x2, waiting for transfers between devices, body(): lax.all_to_all(packed, 'gx', split_axis=0, concat_axis=0, tiled=True)  55.9 us
    pallas_call x2, Pallas kernels, down(): pl.pallas_call(functools.partial(down_kernel, chunk, before is None, last...  26.3 us
    all_to_all x2, starting transfers between devices, body(): lax.all_to_all(packed, 'gx', split_axis=0, concat_axis=0, tiled=True)  18.6 us
    ppermute x2, starting transfers between devices, neighbours(): lax.ppermute(block, axis, forward)  7.44 us
    pallas_call x1, Pallas kernels, pack(): pl.pallas_call(functools.partial(pack_kernel, chunk), out_shape=jax.Shape...  6.13 us
    pallas_call x1, Pallas kernels, prep(): pl.pallas_call(prep_kernel, out_shape=(jax.ShapeDtypeStruct((VOX, 128), F...  5.84 us
  transfers between devices with their start and end apart: 7, of which 6 were waited for; matrix products, arithmetic and copies ran while one was open for 2% of the time, Pallas kernels for 10%

profile of v3, /device:TPU:8, one launch (start us, length us, event | category | flops | bytes accessed | tf_op | source)
XLA Modules:
  0.0 260.8 jit_solution(6424887151394110948)
XLA Ops:
  0.6 5.8 %prep.1 = (f32[6144,128]{1,0:T(8,128)}, f32[256,128]{1,0:T(8,128)}) custom-call(f32[64,6144]{1,0:T(8,128)} %bitcast.21, s32[1,512]{1,0:T(1,128)} %bitcast.30), custom_call_target="tpu_custom_call" | custom-call | tf_op jit(solution)/shard_map/prep/pallas_call | solution.py:94
  6.5 0.0 copy-start.7
  6.5 4.0 %collective-permute-start = (f32[256,128]{1,0:T(8,128)}, f32[256,128]{1,0:T(8,128)S(1)}, u32[]{:S(2)}, u32[]{:S(2)}) collective-permute-start(f32[256,128]{1,0:T(8,128)} %get-tuple-element.21), channel_id=1, source_target_pairs={{0,8},{8,16},{16,24},{24,32},{32,40},{40,48},{48,56},{56,64},{64,7... | collective-permute-start | bytes 393224 | tf_op jit(solution)/shard_map/ppermute | solution.py:440
  10.5 1.3 collective-permute-start.1
  11.8 1.0 copy.16.down_ref
  12.8 3.3 %weights.1 = (bf16[14,256,128]{2,1,0:T(8,128)(2,1)}, bf16[2,4,128,256]{3,2,1,0:T(8,128)(2,1)}, f32[8,128]{1,0:T(8,128)}) custom-call(f32[27,64,64]{2,1,0:T(8,128)} %conv_ref.1, f32[8,128,64]{2,1,0:T(8,128)} %copy.16.down_ref, f32[1,64]{1,0:T(1,128)} %bitcast.31, f32[1,64]{1,0:T(1,128)} %bitcast.32, f32[1,128]{1,0:T(1,128)} %bitcast.33, f32[1,128]{1,0:T(1,128)} %bitcast.34), custom_call_target="tpu_custom_call" | custom-call | bytes 10485760 | tf_op jit(solution)/shard_map/weights/pallas_call | solution.py:474
  16.1 1.7 collective-permute-done.1
  17.8 3.5 %collective-permute-start.2 = (f32[3,256,128]{2,1,0:T(8,128)S(1)}, f32[3,256,128]{2,1,0:T(8,128)S(1)}, u32[]{:S(2)}, u32[]{:S(2)}) collective-permute-start(f32[3,256,128]{2,1,0:T(8,128)S(1)} %pad_maximum_fusion.1), channel_id=1, source_target_pairs={{0,2},{2,4},{4,6},{1,3},{3,5},{5,7},{8,10},{10,12},{12,14},{9,11},... | collective-permute-start | bytes 1179656 | tf_op jit(solution)/shard_map/ppermute | solution.py:440
  21.2 2.4 collective-permute-start.3
  23.6 0.8 reduce
  24.4 0.9 reshape_squeeze.12.ins_ref
  25.3 0.8 reduce.1
  26.1 0.9 reshape_squeeze.13.outs_ref
  27.0 2.5 collective-permute-done.2
  29.5 3.2 %collective-permute-done.3 = f32[3,256,128]{2,1,0:T(8,128)S(1)} collective-permute-done((f32[3,256,128]{2,1,0:T(8,128)S(1)}, f32[3,256,128]{2,1,0:T(8,128)S(1)}, u32[]{:S(2)}, u32[]{:S(2)}) %collective-permute-start.3) | collective-permute-done | bytes 393248 | tf_op jit(solution)/shard_map/ppermute | solution.py:440
  32.7 0.1 pad_maximum_fusion
  32.8 0.1 copy.17
  32.9 0.1 collective-permute-start.4
  33.0 0.6 copy-done.8
  33.6 0.6 copy.18.table_ref
  34.2 1.6 collective-permute-done.4.far_in_ref
  35.9 1.0 copy-done.3
  36.9 115.4 %conv.1 = (f32[64,6144]{1,0:T(8,128)}, f32[6152,128]{1,0:T(8,128)}, f32[32,144,128]{2,1,0:T(8,128)}) custom-call(s32[1]{0:T(128)} %bitcast.place_ref, f32[6144,128]{1,0:T(8,128)} %get-tuple-element.20.own_ref, f32[9,256,128]{2,1,0:T(8,128)} %bitcast.19, f32[9,256,128]{2,1,0:T(8,128)} %copy-done.3, s32[13,2,4,6,128]{4,3,2,1,0:T(8,128)} %reshape_squeeze.12.ins_ref, ...), custom_call_target="tpu_custom_call" | custom-call | tf_op jit(solution)/shard_map/conv/pallas_call | solution.py:294
  152.3 12.1 %all-to-all-start.1 = ((f32[32,144,128]{2,1,0:T(8,128)}), f32[32,144,128]{2,1,0:T(8,128)S(1)}, u32[]{:S(2)}, u32[]{:S(2)}) async-start(f32[32,144,128]{2,1,0:T(8,128)} %get-tuple-element.37), calls=%async_computation.1 | async-start | bytes 4718592 | tf_op jit(solution)/shard_map/all_to_all | solution.py:536
  164.4 6.1 %pack3.1 = f32[32,48,128]{2,1,0:T(8,128)} custom-call(f32[6152,128]{1,0:T(8,128)} %get-tuple-element.34.rows_ref, s32[4,8,3,128]{3,2,1,0:T(4,128)} %copy.18.table_ref), custom_call_target="tpu_custom_call" | custom-call | bytes 10485760 | tf_op jit(solution)/shard_map/pack3/pallas_call | solution.py:334
  170.6 49.5 %all-to-all-done.1.args_0_ = f32[32,144,128]{2,1,0:T(8,128)S(1)} async-done(((f32[32,144,128]{2,1,0:T(8,128)}), f32[32,144,128]{2,1,0:T(8,128)S(1)}, u32[]{:S(2)}, u32[]{:S(2)}) %all-to-all-start.1) | async-done | bytes 2359328 | tf_op jit(solution)/shard_map/all_to_all | solution.py:536
  220.1 6.5 %all-to-all-start = ((f32[32,48,128]{2,1,0:T(8,128)}), f32[32,48,128]{2,1,0:T(8,128)S(1)}, u32[]{:S(2)}, u32[]{:S(2)}) async-start(f32[32,48,128]{2,1,0:T(8,128)} %pack3.1), calls=%async_computation | async-start | bytes 1572864 | tf_op jit(solution)/shard_map/all_to_all | solution.py:536
  226.6 0.7 copy.21.args_1_
  227.2 16.3 %down0.1.args_4_ = f32[3072,128]{1,0:T(8,128)} custom-call(f32[32,144,128]{2,1,0:T(8,128)} %copy-done, s32[4,8,3,128]{3,2,1,0:T(4,128)} %copy.21.args_1_, bf16[2,4,128,256]{3,2,1,0:T(8,128)(2,1)} %get-tuple-element.36.args_2_, f32[8,128]{1,0:T(8,128)} %get-tuple-element.31.norm_ref.args_3_), custom_call_target="tpu_custom_call" | custom-call | bytes 20971520 | tf_op jit(solution)/shard_map/down0/pallas_call | solution.py:421
  243.5 6.4 %all-to-all-done.args_0_ = f32[32,48,128]{2,1,0:T(8,128)S(1)} async-done(((f32[32,48,128]{2,1,0:T(8,128)}), f32[32,48,128]{2,1,0:T(8,128)S(1)}, u32[]{:S(2)}, u32[]{:S(2)}) %all-to-all-start) | async-done | bytes 786464 | tf_op jit(solution)/shard_map/all_to_all | solution.py:536
  249.9 0.9 copy-done.2
  250.8 10.0 %down3.1 = f32[128,3072]{1,0:T(8,128)} custom-call(f32[32,48,128]{2,1,0:T(8,128)} %copy-done.2, s32[4,8,3,128]{3,2,1,0:T(4,128)} %copy.21.args_1_, bf16[2,4,128,256]{3,2,1,0:T(8,128)(2,1)} %get-tuple-element.36.args_2_, f32[8,128]{1,0:T(8,128)} %get-tuple-element.31.norm_ref.args_3_, f32[3072,128]{1,0:T(8,128)} %down0.1.args_4_), custom_call_target="tpu_custom_call" | custom-call | bytes 20971520 | tf_op jit(solution)/shard_map/down3/pallas_call | solution.py:421
  (18 shorter events, 0.1 us)
Async XLA Ops:
  0.6 11.2 %copy-start.6 = (f32[8,128,64]{1,2,0:T(8,128)S(1)}, f32[8,128,64]{1,2,0:T(8,128)}, u32[]{:S(2)}) copy-start(f32[8,128,64]{1,2,0:T(8,128)} %param.21) | copy-start | bytes 786436
  6.5 11.2 %copy-start.7 = (f32[256,128]{1,0:T(8,128)S(1)}, f32[256,128]{1,0:T(8,128)}, u32[]{:S(2)}) copy-start(f32[256,128]{1,0:T(8,128)} %get-tuple-element.21) | copy-start | bytes 393220
  6.5 17.1 %copy-start.4 = (s32[1,1,1,26,3072]{4,2,3,1,0:T(1,128)S(1)}, s32[1,1,1,26,3072]{4,2,3,1,0:T(1,128)}, u32[]{:S(2)}) copy-start(s32[1,1,1,26,3072]{4,2,3,1,0:T(1,128)} %param.14) | copy-start | bytes 958468
  6.5 9.5 %collective-permute-start = (f32[256,128]{1,0:T(8,128)}, f32[256,128]{1,0:T(8,128)S(1)}, u32[]{:S(2)}, u32[]{:S(2)}) collective-permute-start(f32[256,128]{1,0:T(8,128)} %get-tuple-element.21), channel_id=1, source_target_pairs={{0,8},{8,16},{16,24},{24,32},{32,40},{40,48},{48,56},{56,64},{64,7... | collective-permute-start | bytes 393224 | tf_op jit(solution)/shard_map/ppermute | solution.py:440
  10.5 7.2 %collective-permute-start.1 = (f32[256,128]{1,0:T(8,128)}, f32[256,128]{1,0:T(8,128)S(1)}, u32[]{:S(2)}, u32[]{:S(2)}) collective-permute-start(f32[256,128]{1,0:T(8,128)} %get-tuple-element.21), channel_id=1, source_target_pairs={{8,0},{16,8},{24,16},{32,24},{40,32},{48,40},{56,48},{64,56},{72,6... | collective-permute-start | bytes 393224 | tf_op jit(solution)/shard_map/ppermute | solution.py:440
  12.8 12.6 %copy-start.5 = (s32[1,1,1,26,3072]{4,2,3,1,0:T(1,128)S(1)}, s32[1,1,1,26,3072]{4,2,3,1,0:T(1,128)}, u32[]{:S(2)}) copy-start(s32[1,1,1,26,3072]{4,2,3,1,0:T(1,128)} %param.15) | copy-start | bytes 958468
  17.8 11.8 %collective-permute-start.2 = (f32[3,256,128]{2,1,0:T(8,128)S(1)}, f32[3,256,128]{2,1,0:T(8,128)S(1)}, u32[]{:S(2)}, u32[]{:S(2)}) collective-permute-start(f32[3,256,128]{2,1,0:T(8,128)S(1)} %pad_maximum_fusion.1), channel_id=1, source_target_pairs={{0,2},{2,4},{4,6},{1,3},{3,5},{5,7},{8,10},{10,12},{12,14},{9,11},... | collective-permute-start | bytes 1179656 | tf_op jit(solution)/shard_map/ppermute | solution.py:440
  21.2 11.5 %collective-permute-start.3 = (f32[3,256,128]{2,1,0:T(8,128)S(1)}, f32[3,256,128]{2,1,0:T(8,128)S(1)}, u32[]{:S(2)}, u32[]{:S(2)}) collective-permute-start(f32[3,256,128]{2,1,0:T(8,128)S(1)} %pad_maximum_fusion.1), channel_id=1, source_target_pairs={{2,0},{4,2},{6,4},{3,1},{5,3},{7,5},{10,8},{12,10},{14,12},{11,9},... | collective-permute-start | bytes 1179656 | tf_op jit(solution)/shard_map/ppermute | solution.py:440
  32.8 0.8 copy-start.8
  32.9 3.0 %copy-start.1 = (f32[3,3,256,128]{3,2,1,0:T(8,128)}, f32[3,3,256,128]{3,2,1,0:T(8,128)S(1)}, u32[]{:S(2)}) copy-start(f32[3,3,256,128]{3,2,1,0:T(8,128)S(1)} %copy.17) | copy-start | bytes 3538948
  32.9 2.9 %collective-permute-start.4 = (f32[9,256,128]{2,1,0:T(8,128)S(1)}, f32[9,256,128]{2,1,0:T(8,128)S(1)}, u32[]{:S(2)}, u32[]{:S(2)}) collective-permute-start(f32[9,256,128]{2,1,0:T(8,128)S(1)} %bitcast.18), channel_id=1, source_target_pairs={{0,1},{1,0},{2,3},{3,2},{4,5},{5,4},{6,7},{7,6},{8,9},{9,8},{10,11... | collective-permute-start | bytes 3538952 | tf_op jit(solution)/shard_map/ppermute | solution.py:519
  35.9 1.0 copy-start.3
  152.3 67.8 %all-to-all-start.1 = ((f32[32,144,128]{2,1,0:T(8,128)}), f32[32,144,128]{2,1,0:T(8,128)S(1)}, u32[]{:S(2)}, u32[]{:S(2)}) async-start(f32[32,144,128]{2,1,0:T(8,128)} %get-tuple-element.37), calls=%async_computation.1 | async-start | bytes 4718592 | tf_op jit(solution)/shard_map/all_to_all | solution.py:536
  170.5 56.0 %copy-start.9 = (s32[1,1,1,32,384]{4,3,2,1,0:T(8,128)S(1)}, s32[1,1,1,32,384]{4,3,2,1,0:T(8,128)}, u32[]{:S(2)}) copy-start(s32[1,1,1,32,384]{4,3,2,1,0:T(8,128)} %param.17) | copy-start | bytes 147460
  220.1 7.1 %copy-start = (f32[32,144,128]{2,1,0:T(8,128)}, f32[32,144,128]{2,1,0:T(8,128)S(1)}, u32[]{:S(2)}) copy-start(f32[32,144,128]{2,1,0:T(8,128)S(1)} %all-to-all-done.1.args_0_) | copy-start | bytes 7077892
  220.1 29.8 %all-to-all-start = ((f32[32,48,128]{2,1,0:T(8,128)}), f32[32,48,128]{2,1,0:T(8,128)S(1)}, u32[]{:S(2)}, u32[]{:S(2)}) async-start(f32[32,48,128]{2,1,0:T(8,128)} %pack3.1), calls=%async_computation | async-start | bytes 1572864 | tf_op jit(solution)/shard_map/all_to_all | solution.py:536
  249.9 0.9 copy-start.2

commit v4 on v3

--- a/solution.py
+++ b/solution.py
@@ -134,7 +134,7 @@
     return table.reshape(TABLES, SPLIT, CAP // 128, 128)
 
 
-def pack_rows(chunk, rows_ref, refs, out_ref):
+def pack_rows(chunk, rows_ref, refs, out_ref, low_owner=0, high_owner=SPLIT):
     start, groups = chunk
     low = low_lanes()
 
@@ -148,7 +148,7 @@
                 out_ref[a + part * SPLIT, pl.ds(u, 1), :] = jnp.where(low, first, second)
         return carry
 
-    lax.fori_loop(0, SPLIT, owner, 0)
+    lax.fori_loop(low_owner, high_owner, owner, 0)
 
 
 def conv_kernel(
@@ -282,10 +282,18 @@
         copy.wait()
     for copy in outgoing:
         copy.start()
-    pack_rows(CHUNKS[0], acc_ref, slot_refs, packed_ref)
-    packed = pltpu.make_async_copy(packed_ref, packed_out_ref, out_sem.at[2])
-    packed.start()
-    for copy in (*outgoing, packed):
+    for i in range(2):
+        low_owner, high_owner = i * SPLIT // 2, (i + 1) * SPLIT // 2
+        pack_rows(CHUNKS[0], acc_ref, slot_refs, packed_ref, low_owner, high_owner)
+        for part in range(TABLES):
+            at = pl.ds(part * SPLIT + low_owner, SPLIT // 2)
+            outgoing.append(
+                pltpu.make_async_copy(
+                    packed_ref.at[at], packed_out_ref.at[at], out_sem.at[2 + i * TABLES + part]
+                )
+            )
+            outgoing[-1].start()
+    for copy in outgoing:
         copy.wait()
 
 
@@ -311,7 +319,7 @@
             pltpu.VMEM((9, BND // 2, 128), F32),
             pltpu.VMEM((STEPS + 1, 256, 128), BF16),
             pltpu.SemaphoreType.DMA((4,)),
-            pltpu.SemaphoreType.DMA((3,)),
+            pltpu.SemaphoreType.DMA((2 + 2 * TABLES,)),
             pltpu.SemaphoreType.DMA((2, 4 * CUTS)),
         ]
         + [pltpu.SMEM((2, BLOCKS, 128), jnp.int32)] * (4 * CUTS)
@@ -344,17 +352,22 @@
 
 
 def down_kernel(chunk, first, last, *args):
-    x_ref, cols_ref, w_ref, norm_ref, *rest = args
+    x_in_ref, cols_ref, w_in_ref, norm_ref, *rest = args
     if not first:
         before_in_ref, *rest, before_ref, before_sem = rest
         before_copy = pltpu.make_async_copy(before_in_ref, before_ref, before_sem)
         before_copy.start()
     out_ref, sem, *rest = rest
-    refs, (p0_ref, p1_ref, *z_refs) = rest[:TABLES], rest[TABLES:]
+    refs, rest = rest[:TABLES], rest[TABLES:]
+    x_ref, w_ref, result_ref, in_sem, out_sem, p0_ref, p1_ref, *z_refs = rest
     copies = slot_tables(cols_ref, sem, refs)
     for copy in copies:
         copy.start()
     start, groups = chunk
+    x_copy = pltpu.make_async_copy(x_in_ref, x_ref, in_sem.at[0])
+    w_copy = pltpu.make_async_copy(w_in_ref.at[:, pl.ds(start, groups)], w_ref, in_sem.at[1])
+    x_copy.start()
+    w_copy.start()
 
     def clear(t, carry):
         at = pl.ds(pl.multiple_of(t * 128, 128), 128)
@@ -363,14 +376,16 @@
         return carry
 
     lax.fori_loop(0, COARSE // 128, clear, 0)
+    x_copy.wait()
+    w_copy.wait()
     for g in range(groups):
 
         def multiply(i, carry):
             x = x_ref[pl.ds(i * 8, 8), pl.ds(g * GROUP, GROUP), :].reshape(8 * GROUP, 128)
             hi, lo = split(x)
-            part = jnp.dot(hi, w_ref[0, start + g], preferred_element_type=F32)
-            part += jnp.dot(lo, w_ref[0, start + g], preferred_element_type=F32)
-            part += jnp.dot(hi, w_ref[1, start + g], preferred_element_type=F32)
+            part = jnp.dot(hi, w_ref[0, g], preferred_element_type=F32)
+            part += jnp.dot(lo, w_ref[0, g], preferred_element_type=F32)
+            part += jnp.dot(hi, w_ref[1, g], preferred_element_type=F32)
             at = pl.ds(pl.multiple_of((g * OWNERS + i * 8) * GROUP, 8 * GROUP), 8 * GROUP)
             p0_ref[at, :] = part[:, :128]
             p1_ref[at, :] = part[:, 128:]
@@ -407,12 +422,20 @@
         if not first:
             total = total + before_ref[at, :]
         if last:
-            out_ref[:, at] = jnp.maximum(norm_ref[2:3, :] * total + norm_ref[3:4, :], 0.0).T
+            result_ref[:, at] = jnp.maximum(norm_ref[2:3, :] * total + norm_ref[3:4, :], 0.0).T
         else:
-            out_ref[at, :] = total
-        return carry
-
-    lax.fori_loop(0, COARSE // 128, finish, 0)
+            result_ref[at, :] = total
+        return carry
+
+    leaving = []
+    for i in range(4):
+        lax.fori_loop(i * COARSE // 512, (i + 1) * COARSE // 512, finish, 0)
+        piece = pl.ds(i * COARSE // 4, COARSE // 4)
+        at = (slice(None), piece) if last else (piece, slice(None))
+        leaving.append(pltpu.make_async_copy(result_ref.at[at], out_ref.at[at], out_sem.at[i]))
+        leaving[i].start()
+    for copy in leaving:
+        copy.wait()
 
 
 def down(chunk, arrived, cols, weights, norm, before):
@@ -421,9 +444,16 @@
     return pl.pallas_call(
         functools.partial(down_kernel, chunk, before is None, last),
         out_shape=jax.ShapeDtypeStruct((CHO, COARSE) if last else (COARSE, CHO), F32),
-        in_specs=[VMEM, ANY, VMEM, VMEM] + [ANY] * len(carried),
-        out_specs=VMEM,
+        in_specs=[ANY, ANY, ANY, VMEM] + [ANY] * len(carried),
+        out_specs=ANY,
         scratch_shapes=SLOT_SCRATCH
+        + [
+            pltpu.VMEM((OWNERS, chunk[1] * GROUP, 128), F32),
+            pltpu.VMEM((2, chunk[1], 128, 2 * CHO), BF16),
+            pltpu.VMEM((CHO, COARSE) if last else (COARSE, CHO), F32),
+            pltpu.SemaphoreType.DMA((2,)),
+            pltpu.SemaphoreType.DMA((4,)),
+        ]
         + [pltpu.VMEM((OWNERS * chunk[1] * GROUP, 128), F32)] * 2
         + [pltpu.VMEM((COARSE + 8, 128), F32)] * ACCS
         + [pltpu.VMEM((COARSE, CHO), F32), pltpu.SemaphoreType.DMA] * len(carried),

time: 262 us -> 261 us (level)
  no operation moved by 1% of the time
where the time goes in v4:
time: 261 us
  Pallas kernels  156 us (60%)
  waiting for transfers between devices  65.6 us (25%)
  starting transfers between devices  30 us (11%)
  local copies, waits for them, and re-layouts  6.78 us (3%)
    pallas_call x1, Pallas kernels, conv(): pl.pallas_call(conv_kernel, out_shape=(jax.ShapeDtypeStruct((CH, VOX), F3...  115 us
    all_to_all x2, waiting for transfers between devices, body(): lax.all_to_all(packed, 'gx', split_axis=0, concat_axis=0, tiled=True)  56.6 us
    pallas_call x2, Pallas kernels, down(): pl.pallas_call(functools.partial(down_kernel, chunk, before is None, last...  25.5 us
    all_to_all x2, starting transfers between devices, body(): lax.all_to_all(packed, 'gx', split_axis=0, concat_axis=0, tiled=True)  18.8 us
    ppermute x2, starting transfers between devices, neighbours(): lax.ppermute(block, axis, forward)  7.44 us
    pallas_call x1, Pallas kernels, pack(): pl.pallas_call(functools.partial(pack_kernel, chunk), out_shape=jax.Shape...  6.13 us
    pallas_call x1, Pallas kernels, prep(): pl.pallas_call(prep_kernel, out_shape=(jax.ShapeDtypeStruct((VOX, 128), F...  5.84 us
  transfers between devices with their start and end apart: 7, of which 6 were waited for; matrix products, arithmetic and copies ran while one was open for 2% of the time, Pallas kernels for 10%

profile of v4, /device:TPU:8, one launch (start us, length us, event | category | flops | bytes accessed | tf_op | source)
XLA Modules:
  0.0 260.7 jit_solution(2257152534823824894)
XLA Ops:
  0.6 5.8 %prep.1 = (f32[6144,128]{1,0:T(8,128)}, f32[256,128]{1,0:T(8,128)}) custom-call(f32[64,6144]{1,0:T(8,128)} %bitcast.21, s32[1,512]{1,0:T(1,128)} %bitcast.30), custom_call_target="tpu_custom_call" | custom-call | tf_op jit(solution)/shard_map/prep/pallas_call | solution.py:94
  6.5 0.0 copy-start.4
  6.5 4.0 %collective-permute-start = (f32[256,128]{1,0:T(8,128)}, f32[256,128]{1,0:T(8,128)S(1)}, u32[]{:S(2)}, u32[]{:S(2)}) collective-permute-start(f32[256,128]{1,0:T(8,128)} %get-tuple-element.21), channel_id=1, source_target_pairs={{0,8},{8,16},{16,24},{24,32},{32,40},{40,48},{48,56},{56,64},{64,7... | collective-permute-start | bytes 393224 | tf_op jit(solution)/shard_map/ppermute | solution.py:470
  10.5 1.3 collective-permute-start.1
  11.8 1.0 copy.16.down_ref
  12.8 3.3 %weights.1 = (bf16[14,256,128]{2,1,0:T(8,128)(2,1)}, bf16[2,4,128,256]{3,2,1,0:T(8,128)(2,1)}, f32[8,128]{1,0:T(8,128)}) custom-call(f32[27,64,64]{2,1,0:T(8,128)} %conv_ref.1, f32[8,128,64]{2,1,0:T(8,128)} %copy.16.down_ref, f32[1,64]{1,0:T(1,128)} %bitcast.31, f32[1,64]{1,0:T(1,128)} %bitcast.32, f32[1,128]{1,0:T(1,128)} %bitcast.33, f32[1,128]{1,0:T(1,128)} %bitcast.34), custom_call_target="tpu_custom_call" | custom-call | bytes 10485760 | tf_op jit(solution)/shard_map/weights/pallas_call | solution.py:504
  16.1 1.7 collective-permute-done.1
  17.8 3.5 %collective-permute-start.2 = (f32[3,256,128]{2,1,0:T(8,128)S(1)}, f32[3,256,128]{2,1,0:T(8,128)S(1)}, u32[]{:S(2)}, u32[]{:S(2)}) collective-permute-start(f32[3,256,128]{2,1,0:T(8,128)S(1)} %pad_maximum_fusion.1), channel_id=1, source_target_pairs={{0,2},{2,4},{4,6},{1,3},{3,5},{5,7},{8,10},{10,12},{12,14},{9,11},... | collective-permute-start | bytes 1179656 | tf_op jit(solution)/shard_map/ppermute | solution.py:470
  21.2 2.4 collective-permute-start.3
  23.6 0.8 reduce
  24.4 0.9 reshape_squeeze.12.ins_ref
  25.3 0.8 reduce.1
  26.1 0.9 reshape_squeeze.13.outs_ref
  27.0 2.5 collective-permute-done.2
  29.5 3.2 %collective-permute-done.3 = f32[3,256,128]{2,1,0:T(8,128)S(1)} collective-permute-done((f32[3,256,128]{2,1,0:T(8,128)S(1)}, f32[3,256,128]{2,1,0:T(8,128)S(1)}, u32[]{:S(2)}, u32[]{:S(2)}) %collective-permute-start.3) | collective-permute-done | bytes 393248 | tf_op jit(solution)/shard_map/ppermute | solution.py:470
  32.7 0.1 pad_maximum_fusion
  32.8 0.1 copy.17
  32.9 0.1 collective-permute-start.4
  33.0 0.6 copy-done.8
  33.6 0.6 copy.18.table_ref
  34.2 1.6 collective-permute-done.4.far_in_ref
  35.9 1.0 copy-done.3
  36.9 115.0 %conv.1 = (f32[64,6144]{1,0:T(8,128)}, f32[6152,128]{1,0:T(8,128)}, f32[32,144,128]{2,1,0:T(8,128)}) custom-call(s32[1]{0:T(128)} %bitcast.place_ref, f32[6144,128]{1,0:T(8,128)} %get-tuple-element.20.own_ref, f32[9,256,128]{2,1,0:T(8,128)} %bitcast.19, f32[9,256,128]{2,1,0:T(8,128)} %copy-done.3, s32[13,2,4,6,128]{4,3,2,1,0:T(8,128)} %reshape_squeeze.12.ins_ref, ...), custom_call_target="tpu_custom_call" | custom-call | tf_op jit(solution)/shard_map/conv/pallas_call | solution.py:302
  151.9 12.1 %all-to-all-start.1 = ((f32[32,144,128]{2,1,0:T(8,128)}), f32[32,144,128]{2,1,0:T(8,128)S(1)}, u32[]{:S(2)}, u32[]{:S(2)}) async-start(f32[32,144,128]{2,1,0:T(8,128)} %get-tuple-element.37), calls=%async_computation.1 | async-start | bytes 4718592 | tf_op jit(solution)/shard_map/all_to_all | solution.py:566
  164.0 6.1 %pack3.1 = f32[32,48,128]{2,1,0:T(8,128)} custom-call(f32[6152,128]{1,0:T(8,128)} %get-tuple-element.34.rows_ref, s32[4,8,3,128]{3,2,1,0:T(4,128)} %copy.18.table_ref), custom_call_target="tpu_custom_call" | custom-call | bytes 10485760 | tf_op jit(solution)/shard_map/pack3/pallas_call | solution.py:342
  170.1 49.6 %all-to-all-done.1.args_0_ = f32[32,144,128]{2,1,0:T(8,128)S(1)} async-done(((f32[32,144,128]{2,1,0:T(8,128)}), f32[32,144,128]{2,1,0:T(8,128)S(1)}, u32[]{:S(2)}, u32[]{:S(2)}) %all-to-all-start.1) | async-done | bytes 2359328 | tf_op jit(solution)/shard_map/all_to_all | solution.py:566
  219.8 6.8 %all-to-all-start = ((f32[32,48,128]{2,1,0:T(8,128)}), f32[32,48,128]{2,1,0:T(8,128)S(1)}, u32[]{:S(2)}, u32[]{:S(2)}) async-start(f32[32,48,128]{2,1,0:T(8,128)} %pack3.1), calls=%async_computation | async-start | bytes 1572864 | tf_op jit(solution)/shard_map/all_to_all | solution.py:566
  226.6 0.7 copy.21.args_1_
  227.2 15.6 %down0.1.args_4_ = f32[3072,128]{1,0:T(8,128)} custom-call(f32[32,144,128]{2,1,0:T(8,128)} %copy-done, s32[4,8,3,128]{3,2,1,0:T(4,128)} %copy.21.args_1_, bf16[2,4,128,256]{3,2,1,0:T(8,128)(2,1)} %get-tuple-element.36.args_2_, f32[8,128]{1,0:T(8,128)} %get-tuple-element.31.norm_ref.args_3_), custom_call_target="tpu_custom_call" | custom-call | bytes 20971520 | tf_op jit(solution)/shard_map/down0/pallas_call | solution.py:444
  242.9 6.9 %all-to-all-done.args_0_ = f32[32,48,128]{2,1,0:T(8,128)S(1)} async-done(((f32[32,48,128]{2,1,0:T(8,128)}), f32[32,48,128]{2,1,0:T(8,128)S(1)}, u32[]{:S(2)}, u32[]{:S(2)}) %all-to-all-start) | async-done | bytes 786464 | tf_op jit(solution)/shard_map/all_to_all | solution.py:566
  249.8 0.9 copy-done.2
  250.7 9.8 %down3.1 = f32[128,3072]{1,0:T(8,128)} custom-call(f32[32,48,128]{2,1,0:T(8,128)} %copy-done.2, s32[4,8,3,128]{3,2,1,0:T(4,128)} %copy.21.args_1_, bf16[2,4,128,256]{3,2,1,0:T(8,128)(2,1)} %get-tuple-element.36.args_2_, f32[8,128]{1,0:T(8,128)} %get-tuple-element.31.norm_ref.args_3_, f32[3072,128]{1,0:T(8,128)} %down0.1.args_4_), custom_call_target="tpu_custom_call" | custom-call | bytes 20971520 | tf_op jit(solution)/shard_map/down3/pallas_call | solution.py:444
  (18 shorter events, 0.1 us)
Async XLA Ops:
  0.6 11.2 %copy-start.6 = (f32[8,128,64]{1,2,0:T(8,128)S(1)}, f32[8,128,64]{1,2,0:T(8,128)}, u32[]{:S(2)}) copy-start(f32[8,128,64]{1,2,0:T(8,128)} %param.21) | copy-start | bytes 786436
  6.5 11.2 %copy-start.7 = (f32[256,128]{1,0:T(8,128)S(1)}, f32[256,128]{1,0:T(8,128)}, u32[]{:S(2)}) copy-start(f32[256,128]{1,0:T(8,128)} %get-tuple-element.21) | copy-start | bytes 393220
  6.5 17.1 %copy-start.4 = (s32[1,1,1,26,3072]{4,2,3,1,0:T(1,128)S(1)}, s32[1,1,1,26,3072]{4,2,3,1,0:T(1,128)}, u32[]{:S(2)}) copy-start(s32[1,1,1,26,3072]{4,2,3,1,0:T(1,128)} %param.14) | copy-start | bytes 958468
  6.5 9.5 %collective-permute-start = (f32[256,128]{1,0:T(8,128)}, f32[256,128]{1,0:T(8,128)S(1)}, u32[]{:S(2)}, u32[]{:S(2)}) collective-permute-start(f32[256,128]{1,0:T(8,128)} %get-tuple-element.21), channel_id=1, source_target_pairs={{0,8},{8,16},{16,24},{24,32},{32,40},{40,48},{48,56},{56,64},{64,7... | collective-permute-start | bytes 393224 | tf_op jit(solution)/shard_map/ppermute | solution.py:470
  10.5 7.2 %collective-permute-start.1 = (f32[256,128]{1,0:T(8,128)}, f32[256,128]{1,0:T(8,128)S(1)}, u32[]{:S(2)}, u32[]{:S(2)}) collective-permute-start(f32[256,128]{1,0:T(8,128)} %get-tuple-element.21), channel_id=1, source_target_pairs={{8,0},{16,8},{24,16},{32,24},{40,32},{48,40},{56,48},{64,56},{72,6... | collective-permute-start | bytes 393224 | tf_op jit(solution)/shard_map/ppermute | solution.py:470
  12.8 12.6 %copy-start.5 = (s32[1,1,1,26,3072]{4,2,3,1,0:T(1,128)S(1)}, s32[1,1,1,26,3072]{4,2,3,1,0:T(1,128)}, u32[]{:S(2)}) copy-start(s32[1,1,1,26,3072]{4,2,3,1,0:T(1,128)} %param.15) | copy-start | bytes 958468
  17.8 11.8 %collective-permute-start.2 = (f32[3,256,128]{2,1,0:T(8,128)S(1)}, f32[3,256,128]{2,1,0:T(8,128)S(1)}, u32[]{:S(2)}, u32[]{:S(2)}) collective-permute-start(f32[3,256,128]{2,1,0:T(8,128)S(1)} %pad_maximum_fusion.1), channel_id=1, source_target_pairs={{0,2},{2,4},{4,6},{1,3},{3,5},{5,7},{8,10},{10,12},{12,14},{9,11},... | collective-permute-start | bytes 1179656 | tf_op jit(solution)/shard_map/ppermute | solution.py:470
  21.2 11.5 %collective-permute-start.3 = (f32[3,256,128]{2,1,0:T(8,128)S(1)}, f32[3,256,128]{2,1,0:T(8,128)S(1)}, u32[]{:S(2)}, u32[]{:S(2)}) collective-permute-start(f32[3,256,128]{2,1,0:T(8,128)S(1)} %pad_maximum_fusion.1), channel_id=1, source_target_pairs={{2,0},{4,2},{6,4},{3,1},{5,3},{7,5},{10,8},{12,10},{14,12},{11,9},... | collective-permute-start | bytes 1179656 | tf_op jit(solution)/shard_map/ppermute | solution.py:470
  32.8 0.8 copy-start.8
  32.9 3.0 %copy-start.1 = (f32[3,3,256,128]{3,2,1,0:T(8,128)}, f32[3,3,256,128]{3,2,1,0:T(8,128)S(1)}, u32[]{:S(2)}) copy-start(f32[3,3,256,128]{3,2,1,0:T(8,128)S(1)} %copy.17) | copy-start | bytes 3538948
  32.9 2.9 %collective-permute-start.4 = (f32[9,256,128]{2,1,0:T(8,128)S(1)}, f32[9,256,128]{2,1,0:T(8,128)S(1)}, u32[]{:S(2)}, u32[]{:S(2)}) collective-permute-start(f32[9,256,128]{2,1,0:T(8,128)S(1)} %bitcast.18), channel_id=1, source_target_pairs={{0,1},{1,0},{2,3},{3,2},{4,5},{5,4},{6,7},{7,6},{8,9},{9,8},{10,11... | collective-permute-start | bytes 3538952 | tf_op jit(solution)/shard_map/ppermute | solution.py:549
  35.9 1.0 copy-start.3
  151.9 67.9 %all-to-all-start.1 = ((f32[32,144,128]{2,1,0:T(8,128)}), f32[32,144,128]{2,1,0:T(8,128)S(1)}, u32[]{:S(2)}, u32[]{:S(2)}) async-start(f32[32,144,128]{2,1,0:T(8,128)} %get-tuple-element.37), calls=%async_computation.1 | async-start | bytes 4718592 | tf_op jit(solution)/shard_map/all_to_all | solution.py:566
  170.1 56.4 %copy-start.9 = (s32[1,1,1,32,384]{4,3,2,1,0:T(8,128)S(1)}, s32[1,1,1,32,384]{4,3,2,1,0:T(8,128)}, u32[]{:S(2)}) copy-start(s32[1,1,1,32,384]{4,3,2,1,0:T(8,128)} %param.17) | copy-start | bytes 147460
  219.8 7.4 %copy-start = (f32[32,144,128]{2,1,0:T(8,128)}, f32[32,144,128]{2,1,0:T(8,128)S(1)}, u32[]{:S(2)}) copy-start(f32[32,144,128]{2,1,0:T(8,128)S(1)} %all-to-all-done.1.args_0_) | copy-start | bytes 7077892
  219.8 30.0 %all-to-all-start = ((f32[32,48,128]{2,1,0:T(8,128)}), f32[32,48,128]{2,1,0:T(8,128)S(1)}, u32[]{:S(2)}, u32[]{:S(2)}) async-start(f32[32,48,128]{2,1,0:T(8,128)} %pack3.1), calls=%async_computation | async-start | bytes 1572864 | tf_op jit(solution)/shard_map/all_to_all | solution.py:566
  249.8 0.9 copy-start.2
